TPU v7x, 32 devices: a whole 2x2x4 slice. The times are simulated.
32 devices in a mesh: dp: 8 (over z, x), mp: 4 (over y, core).
Axes of the slice: x: 2, y: 2, z: 4, core: 2. Of those that a mesh axis runs over, the one named last changes fastest.
Arguments:
- patches: bfloat16 [8192, 768], P('dp'), may hold values from -6 to 6
- patch_keep: int32 [8, 1024], P('dp'), may hold values 0 or 1
- patch_segment: int32 [8, 1024], P('dp'), may hold values from 0 to 7, never falling along the last dimension, each value on 1 to 256 neighbouring positions
- cotangent: bfloat16 [8192, 768], P('dp'), may hold values from -6 to 6
- w_qkv: bfloat16 [2, 3, 768, 768], P(None, None, None, 'mp'), may hold values from -0.21875 to 0.21875
- w_out: bfloat16 [2, 768, 768], P(None, 'mp'), may hold values from -1.75 to 1.75
- w_up: bfloat16 [2, 768, 3072], P(None, None, 'mp'), may hold values from -0.21875 to 0.21875
- w_down: bfloat16 [2, 3072, 768], P(None, 'mp'), may hold values from -0.109375 to 0.109375
- head_vectors: float32 [2, 6, 768], P(None, None, 'mp'), may hold values from -0.75 to 0.75
- up_bias: float32 [2, 3072], P(None, 'mp'), may hold values from -0.75 to 0.75
- row_vectors: float32 [2, 6, 768], replicated, may hold values from -0.75 to 0.75
Outputs:
- packed_out: bfloat16 [8192, 768], P('dp')
- grad_patches: float32 [8192, 768], P('dp')
- grad_qkv: float32 [2, 3, 768, 768], P(None, None, 'dp', 'mp')
- grad_out: float32 [2, 768, 768], P(None, 'mp', 'dp')
- grad_up: float32 [2, 768, 3072], P(None, 'dp', 'mp')
- grad_down: float32 [2, 3072, 768], P(None, 'mp', 'dp')
- grad_head_vectors: float32 [2, 6, 768], P(None, None, ('mp', 'dp'))
- grad_up_bias: float32 [2, 3072], P(None, ('mp', 'dp'))
- grad_row_vectors: float32 [2, 6, 768], P(None, None, 'dp')
Inputs may be any that keep to these rules, and one draw needn't show every extreme that they name: `patch_segment`: along each row the image numbers never fall; each of the 8 images has 1 to 256 patches.
All inputs are finite; a program needn't handle non-finite values. No bound on the sum of `patch_keep` on one device may be relied on, other than what follows from the above.
Results may differ from a plain program's by a relative error of at most 0.013.
Values sent between devices are 32-bit elements; how exact they have to be, the bound alone decides.
A program may use at most 192 MiB of HBM per device.

v0:
```python
import jax
import jax.numpy as jnp
from jax import lax
from jax.sharding import PartitionSpec as P

HEAD = 64


EPS = 1e-06


def norm_rows(values):
    center = values - jnp.mean(values, axis=-1, keepdims=True)
    rstd = lax.rsqrt(jnp.mean(center * center, axis=-1, keepdims=True) + EPS)
    return (center * rstd, rstd)


def norm_back(grad_hat, x_hat, rstd):
    mean_grad = jnp.mean(grad_hat, axis=-1, keepdims=True)
    mean_cross = jnp.mean(grad_hat * x_hat, axis=-1, keepdims=True)
    return rstd * (grad_hat - mean_grad - x_hat * mean_cross)


def contract_rows(left, right):
    return lax.dot_general(
        left, right, (((0,), (0,)), ((), ())), preferred_element_type=jnp.float32
    )


def contract_cols(left, right):
    return lax.dot_general(
        left, right, (((1,), (1,)), ((), ())), preferred_element_type=jnp.float32
    )


def masked_scores(query, keys, same_image):
    scores = jnp.einsum("qhe,khe->hqk", query, keys, preferred_element_type=jnp.float32) * HEAD ** (
        -0.5
    )
    return jnp.where(same_image[None], scores, -1e30)


def layer_forward(resid, same_image, params, attn_total, mlp_total):
    w_qkv, w_out, w_up, w_down, head_vec, up_bias, row_vec = params
    length = resid.shape[0]
    heads_here = w_qkv.shape[2] // HEAD
    shaped = (length, heads_here, HEAD)
    hat_one, rstd_one = norm_rows(resid)
    normed = (hat_one * (1.0 + row_vec[0]) + row_vec[1]).astype(jnp.bfloat16)
    raw_qkv = jnp.einsum("sd,kde->kse", normed, w_qkv, preferred_element_type=jnp.float32)
    hat_query, rstd_query = norm_rows((raw_qkv[0] + head_vec[0]).reshape(shaped))
    hat_keys, rstd_keys = norm_rows((raw_qkv[1] + head_vec[1]).reshape(shaped))
    query = (
        hat_query * (1.0 + head_vec[3]).reshape(heads_here, HEAD)
        + head_vec[5].reshape(heads_here, HEAD)
    ).astype(jnp.bfloat16)
    keys = (hat_keys * (1.0 + head_vec[4]).reshape(heads_here, HEAD)).astype(jnp.bfloat16)
    values = (raw_qkv[2] + head_vec[2]).reshape(shaped).astype(jnp.bfloat16)
    scores = masked_scores(query, keys, same_image)
    top_score = jnp.max(scores, axis=-1, keepdims=True)
    expo = jnp.exp(scores - top_score)
    total = jnp.sum(expo, axis=-1, keepdims=True)
    log_total = top_score + jnp.log(total)
    probs = (expo / total).astype(jnp.bfloat16)
    attended = jnp.einsum("hqk,khe->qhe", probs, values, preferred_element_type=jnp.float32)
    attended = attended.reshape(length, heads_here * HEAD).astype(jnp.bfloat16)
    middle = (
        resid
        + attn_total(jnp.dot(attended, w_out, preferred_element_type=jnp.float32))
        + row_vec[4]
    )
    hat_two, rstd_two = norm_rows(middle)
    second = (hat_two * (1.0 + row_vec[2]) + row_vec[3]).astype(jnp.bfloat16)
    before = jnp.dot(second, w_up, preferred_element_type=jnp.float32) + up_bias
    hidden = jax.nn.gelu(before, approximate=False).astype(jnp.bfloat16)
    if mlp_total is None:
        output = middle
    else:
        output = (
            middle
            + mlp_total(jnp.dot(hidden, w_down, preferred_element_type=jnp.float32))
            + row_vec[5]
        )
    stored = (
        hat_one,
        rstd_one,
        normed,
        hat_query,
        rstd_query,
        hat_keys,
        rstd_keys,
        query,
        keys,
        values,
        log_total,
        attended,
        hat_two,
        rstd_two,
        second,
        before,
        hidden,
    )
    return (output, stored)


def layer_backward(grad_resid, same_image, params, stored, mlp_in_total, attn_in_total):
    w_qkv, w_out, w_up, w_down, head_vec, up_bias, row_vec = params
    (
        hat_one,
        rstd_one,
        normed,
        hat_query,
        rstd_query,
        hat_keys,
        rstd_keys,
        query,
        keys,
        values,
        log_total,
        attended,
        hat_two,
        rstd_two,
        second,
        before,
        hidden,
    ) = stored
    length = grad_resid.shape[0]
    heads_here = w_qkv.shape[2] // HEAD
    shaped = (length, heads_here, HEAD)
    grad_mlp = grad_resid.astype(jnp.bfloat16)
    down_bias_grad = jnp.sum(grad_mlp.astype(jnp.float32), axis=0)
    grad_down = contract_rows(hidden, grad_mlp)
    grad_hidden = contract_cols(grad_mlp, w_down)
    unused_value, gelu_back = jax.vjp(lambda inner: jax.nn.gelu(inner, approximate=False), before)
    grad_before = gelu_back(grad_hidden)[0].astype(jnp.bfloat16)
    grad_up = contract_rows(second, grad_before)
    up_bias_grad = jnp.sum(grad_before.astype(jnp.float32), axis=0)
    grad_second = mlp_in_total(contract_cols(grad_before, w_up))
    gain_two_grad = jnp.sum(grad_second * hat_two, axis=0)
    shift_two_grad = jnp.sum(grad_second, axis=0)
    grad_middle = grad_resid + norm_back(grad_second * (1.0 + row_vec[2]), hat_two, rstd_two)
    grad_branch = grad_middle.astype(jnp.bfloat16)
    out_bias_grad = jnp.sum(grad_branch.astype(jnp.float32), axis=0)
    grad_w_out = contract_rows(attended, grad_branch)
    grad_attended = contract_cols(grad_branch, w_out).astype(jnp.bfloat16).reshape(shaped)
    probs = jnp.exp(masked_scores(query, keys, same_image) - log_total)
    probs_low = probs.astype(jnp.bfloat16)
    grad_values = jnp.einsum(
        "hqk,qhe->khe", probs_low, grad_attended, preferred_element_type=jnp.float32
    )
    grad_probs = jnp.einsum(
        "qhe,khe->hqk", grad_attended, values, preferred_element_type=jnp.float32
    )
    grad_scores = probs * (grad_probs - jnp.sum(grad_probs * probs, axis=-1, keepdims=True))
    grad_scores = grad_scores.astype(jnp.bfloat16)
    score_scale = HEAD ** (-0.5)
    grad_query = (
        jnp.einsum("hqk,khe->qhe", grad_scores, keys, preferred_element_type=jnp.float32)
        * score_scale
    )
    grad_keys = (
        jnp.einsum("hqk,qhe->khe", grad_scores, query, preferred_element_type=jnp.float32)
        * score_scale
    )
    query_shift_grad = jnp.sum(grad_query, axis=0).reshape(-1)
    query_gain_grad = jnp.sum(grad_query * hat_query, axis=0).reshape(-1)
    keys_gain_grad = jnp.sum(grad_keys * hat_keys, axis=0).reshape(-1)
    gains_query = (1.0 + head_vec[3]).reshape(heads_here, HEAD)
    gains_keys = (1.0 + head_vec[4]).reshape(heads_here, HEAD)
    raw_query = norm_back(grad_query * gains_query, hat_query, rstd_query).reshape(
        length, heads_here * HEAD
    )
    raw_keys = norm_back(grad_keys * gains_keys, hat_keys, rstd_keys).reshape(
        length, heads_here * HEAD
    )
    raw_values = grad_values.reshape(length, heads_here * HEAD)
    head_grads = jnp.stack(
        [
            jnp.sum(raw_query, axis=0),
            jnp.sum(raw_keys, axis=0),
            jnp.sum(raw_values, axis=0),
            query_gain_grad,
            keys_gain_grad,
            query_shift_grad,
        ]
    )
    grad_raw = jnp.stack([raw_query, raw_keys, raw_values]).astype(jnp.bfloat16)
    grad_qkv = jnp.einsum("sd,kse->kde", normed, grad_raw, preferred_element_type=jnp.float32)
    grad_normed = attn_in_total(
        jnp.einsum("kse,kde->sd", grad_raw, w_qkv, preferred_element_type=jnp.float32)
    )
    gain_one_grad = jnp.sum(grad_normed * hat_one, axis=0)
    shift_one_grad = jnp.sum(grad_normed, axis=0)
    grad_input = grad_middle + norm_back(grad_normed * (1.0 + row_vec[0]), hat_one, rstd_one)
    row_grads = jnp.stack(
        [
            gain_one_grad,
            shift_one_grad,
            gain_two_grad,
            shift_two_grad,
            out_bias_grad,
            down_bias_grad,
        ]
    )
    return (
        grad_input,
        (grad_qkv, grad_w_out, grad_up, grad_down, head_grads, up_bias_grad, row_grads),
    )


def body(
    patches,
    patch_keep,
    patch_segment,
    cotangent,
    w_qkv,
    w_out,
    w_up,
    w_down,
    head_vectors,
    up_bias,
    row_vectors,
):
    keep_row = patch_keep[0]
    segment_row = patch_segment[0]
    slot_count = keep_row.shape[0]
    positions = jnp.arange(slot_count, dtype=jnp.int32)
    slot_index = jnp.cumsum(keep_row) - 1
    target = jnp.where(keep_row > 0, slot_index, slot_count)
    source = jnp.zeros((slot_count,), jnp.int32).at[target].set(positions, mode="drop")
    live_mask = positions < jnp.sum(keep_row)
    live_float = live_mask[:, None].astype(jnp.float32)
    image_slot = jnp.where(live_mask, segment_row[source], -1)
    same_image = image_slot[:, None] == image_slot[None, :]
    resid = jnp.take(patches, source, axis=0).astype(jnp.float32) * live_float
    weights = (w_qkv, w_out, w_up, w_down, head_vectors, up_bias, row_vectors)
    layers = w_qkv.shape[0]
    layer_inputs = []
    stored_all = []
    for layer_index in range(layers):
        params = tuple((item[layer_index] for item in weights))
        layer_inputs.append(resid)
        resid, stored = layer_forward(
            resid,
            same_image,
            params,
            lambda partial_value: lax.psum(partial_value, "mp"),
            lambda partial_value: lax.psum(partial_value, "mp"),
        )
        stored_all.append(stored)
    packed_out = (resid * live_float).astype(jnp.bfloat16)
    grad_resid = cotangent.astype(jnp.float32) * live_float
    layer_grads = [None] * layers
    for layer_index in reversed(range(layers)):
        params = tuple((item[layer_index] for item in weights))
        unused_out, stored = layer_forward(
            layer_inputs[layer_index],
            same_image,
            params,
            lambda partial_value: lax.psum(partial_value, "mp"),
            None,
        )
        grad_resid, grads = layer_backward(
            grad_resid,
            same_image,
            params,
            stored,
            lambda partial_value: lax.psum(partial_value, "mp"),
            lambda partial_value: lax.psum(partial_value, "mp"),
        )
        grads = (
            lax.psum_scatter(grads[0], "dp", scatter_dimension=1, tiled=True),
            lax.psum_scatter(grads[1], "dp", scatter_dimension=1, tiled=True),
            lax.psum_scatter(grads[2], "dp", scatter_dimension=0, tiled=True),
            lax.psum_scatter(grads[3], "dp", scatter_dimension=1, tiled=True),
            lax.psum_scatter(grads[4], "dp", scatter_dimension=1, tiled=True),
            lax.psum_scatter(grads[5], "dp", scatter_dimension=0, tiled=True),
            lax.psum_scatter(grads[6], "dp", scatter_dimension=1, tiled=True),
        )
        layer_grads[layer_index] = grads
    stacked = tuple((jnp.stack([entry[member] for entry in layer_grads]) for member in range(7)))
    clipped = jnp.clip(slot_index, 0, slot_count - 1)
    grad_patches = jnp.take(grad_resid, clipped, axis=0) * keep_row[:, None].astype(jnp.float32)
    return (
        packed_out,
        grad_patches,
        stacked[0],
        stacked[1],
        stacked[2],
        stacked[3],
        stacked[4],
        stacked[5],
        stacked[6],
    )


def solution(mesh):
    return jax.shard_map(
        body,
        mesh=mesh,
        in_specs=(
            P("dp", None),
            P("dp", None),
            P("dp", None),
            P("dp", None),
            P(None, None, None, "mp"),
            P(None, "mp", None),
            P(None, None, "mp"),
            P(None, "mp", None),
            P(None, None, "mp"),
            P(None, "mp"),
            P(),
        ),
        out_specs=(
            P("dp", None),
            P("dp", None),
            P(None, None, "dp", "mp"),
            P(None, "mp", "dp"),
            P(None, "dp", "mp"),
            P(None, "mp", "dp"),
            P(None, None, ("mp", "dp")),
            P(None, ("mp", "dp")),
            P(None, None, "dp"),
        ),
        check_vma=False,
    )
```

profile of v0, /device:TPU:0, one launch (start us, length us, event | category | flops | bytes accessed | tf_op | source)
XLA Modules:
  0.0 1435.1 jit_solution(15972741006851822296)
XLA Ops:
  28.8 4.8 gather_fusion.1
  50.0 70.6 %all-reduce.14.cloned.1.call-done = f32[1024,768]{1,0:T(8,128)} async-done(((f32[1024,768]{1,0:T(8,128)}), f32[1024,768]{1,0:T(8,128)}) %all-reduce.14.cloned.1.call-update) | async-done | bytes 3145744 | tf_op jit(solution)/shard_map/psum | solution.py:247
  125.8 9.7 multiply_convert_fusion.4
  140.5 68.0 %all-reduce.16.cloned.1.call-done = f32[1024,768]{1,0:T(8,128)} async-done(((f32[1024,768]{1,0:T(8,128)}), f32[1024,768]{1,0:T(8,128)}) %all-reduce.16.cloned.1.call-update) | async-done | bytes 3145744 | tf_op jit(solution)/shard_map/psum | solution.py:248
  226.2 68.4 %all-reduce.18.cloned.1.call-done = f32[1024,768]{1,0:T(8,128)} async-done(((f32[1024,768]{1,0:T(8,128)}), f32[1024,768]{1,0:T(8,128)}) %all-reduce.18.cloned.1.call-update) | async-done | bytes 3145744 | tf_op jit(solution)/shard_map/psum | solution.py:247
  300.8 9.9 multiply_convert_fusion.3
  320.8 66.3 %all-reduce.20.cloned.1.call-done = f32[1024,768]{1,0:T(8,128)} async-done(((f32[1024,768]{1,0:T(8,128)}), f32[1024,768]{1,0:T(8,128)}) %all-reduce.20.cloned.1.call-update) | async-done | bytes 3145744 | tf_op jit(solution)/shard_map/psum | solution.py:268
  397.5 10.7 multiply_reduce_fusion.1
  412.3 6.9 multiply_convert_fusion.1
  429.1 68.5 %all-reduce.22.cloned.1.call-done = f32[1024,768]{1,0:T(8,128)} async-done(((f32[1024,768]{1,0:T(8,128)}), f32[1024,768]{1,0:T(8,128)}) %all-reduce.22.cloned.1.call-update) | async-done | bytes 3145744 | tf_op jit(solution)/shard_map/psum | solution.py:269
  516.8 4.8 fusion.48
  521.7 61.3 %all-reduce.24.cloned.1.call-done = f32[1024,768]{1,0:T(8,128)} async-done(((f32[1024,768]{1,0:T(8,128)}), f32[1024,768]{1,0:T(8,128)}) %all-reduce.24.cloned.1.call-update) | async-done | bytes 3145744 | tf_op jit(solution)/shard_map/psum | solution.py:268
  593.5 5.9 multiply_reduce_fusion
  602.1 6.9 multiply_convert_fusion
  623.4 5.6 fusion.35
  641.7 4.8 fusion.134
  646.6 5.2 fusion.115
  652.0 5.5 fusion.153
  662.7 76.7 %all-reduce.26.cloned.1.call-done = (f32[1024,768]{1,0:T(8,128)}, f32[1024,768]{1,0:T(8,128)}) async-done(((f32[1024,768]{1,0:T(8,128)}, f32[1024,768]{1,0:T(8,128)}), (f32[1024,768]{1,0:T(8,128)}, f32[1024,768]{1,0:T(8,128)})) %all-reduce.26.cloned.1.call-update) | async-done | bytes 6291472 | tf_op jit(solution)/shard_map/psum | solution.py:248
  757.0 48.4 %reduce-scatter.39.cloned.1.call-done = f32[96,192]{1,0:T(8,128)} async-done(((f32[768,192]{1,0:T(8,128)}), f32[96,192]{1,0:T(8,128)}) %reduce-scatter.39.cloned.1.call-update) | async-done | bytes 73744
  807.0 35.4 %all-reduce.4 = (f32[6,192]{1,0:T(8,128)S(1)}, f32[6,192]{1,0:T(8,128)S(1)}, f32[768]{0:T(1024)S(1)}, f32[768]{0:T(1024)S(1)}) all-reduce(f32[6,192]{1,0:T(8,128)S(1)} %stack.159, f32[6,192]{1,0:T(8,128)S(1)} %stack.154, f32[768]{0:T(1024)S(1)} %copy-done.164, f32[768]{0:T(1024)S(1)} %copy-done.165), channel_id=11, replica_groups=mesh['dp'=8,'mp'=4] {'dp'}, use_global_device_ids=true, to_apply=%region_71.72.clone | all-reduce | flops 3840 | bytes 30720
  843.8 31.4 %reduce-scatter.35.cloned.1.call-done = f32[96,576]{1,0:T(8,128)} async-done(((f32[768,576]{1,0:T(8,128)}), f32[96,576]{1,0:T(8,128)}) %reduce-scatter.35.cloned.1.call-update) | async-done | bytes 221200
  876.5 63.2 %reduce-scatter.37.cloned.1.call-done = f32[96,192]{1,0:T(8,128)} async-done(((f32[768,192]{1,0:T(8,128)}), f32[96,192]{1,0:T(8,128)}) %reduce-scatter.37.cloned.1.call-update) | async-done | bytes 73744
  941.5 7.1 multiply_add_fusion
  948.6 5.2 gather_fusion.2
  957.9 53.9 %reduce-scatter.31.cloned.1.call-done = f32[768,96]{0,1:T(8,128)} async-done(((f32[768,768]{0,1:T(8,128)}), f32[768,96]{0,1:T(8,128)}) %reduce-scatter.31.cloned.1.call-update) | async-done | bytes 294928 | tf_op jit(solution)/shard_map/reduce_scatter | solution.py:275
  1011.8 71.9 %reduce-scatter.29.cloned.1.call-done = f32[768,96]{0,1:T(8,128)} async-done(((f32[768,768]{0,1:T(8,128)}), f32[768,96]{0,1:T(8,128)}) %reduce-scatter.29.cloned.1.call-update) | async-done | bytes 294928 | tf_op jit(solution)/shard_map/reduce_scatter | solution.py:275
  1085.6 70.2 %reduce-scatter.27.cloned.1.call-done = f32[96,768]{1,0:T(8,128)} async-done(((f32[768,768]{1,0:T(8,128)}), f32[96,768]{1,0:T(8,128)}) %reduce-scatter.27.cloned.1.call-update) | async-done | bytes 294928 | tf_op jit(solution)/shard_map/reduce_scatter | solution.py:274
  1155.8 72.2 %reduce-scatter.25.cloned.1.call-done = f32[96,768]{1,0:T(8,128)} async-done(((f32[768,768]{1,0:T(8,128)}), f32[96,768]{1,0:T(8,128)}) %reduce-scatter.25.cloned.1.call-update) | async-done | bytes 294928 | tf_op jit(solution)/shard_map/reduce_scatter | solution.py:274
  1229.9 62.0 %reduce-scatter.41.cloned.1.call-done = f32[96,6]{1,0:T(8,128)} async-done(((f32[768,6]{1,0:T(8,128)}), f32[96,6]{1,0:T(8,128)}) %reduce-scatter.41.cloned.1.call-update) | async-done | bytes 2320
  1292.8 63.6 %reduce-scatter.43.cloned.1.call-done = f32[96,6]{1,0:T(8,128)} async-done(((f32[768,6]{1,0:T(8,128)}), f32[96,6]{1,0:T(8,128)}) %reduce-scatter.43.cloned.1.call-update) | async-done | bytes 2320
  1357.9 68.1 %reduce-scatter.33.cloned.1.call-done = f32[96,576]{1,0:T(8,128)} async-done(((f32[768,576]{1,0:T(8,128)}), f32[96,576]{1,0:T(8,128)}) %reduce-scatter.33.cloned.1.call-update) | async-done | bytes 221200
  (601 shorter events, 203.8 us)
Async XLA Ops:
  7.2 113.4 %all-reduce.14.cloned.1.call-start = ((), (), s32[]{:S(2)}) async-start(), calls=%async_computation.10 | async-start | bytes 6291456 | tf_op jit(solution)/shard_map/psum | solution.py:247
  14.8 105.8 %copy-start.103 = (pred[1024]{0:T(1024)(128)(4,1)}, pred[1024]{0:T(1024)(128)(4,1)S(1)}, u32[]{:S(2)}) copy-start(pred[1024]{0:T(1024)(128)(4,1)S(1)} %compare_and_fusion.1) | copy-start | bytes 3076
  17.5 293.2 %copy-start.65 = (f32[1024]{0:T(1024)}, f32[1024]{0:T(1024)S(1)}, u32[]{:S(2)}) copy-start(f32[1024]{0:T(1024)S(1)} %fusion.105) | copy-start | bytes 12292
  24.1 100.5 %copy-start.114 = (f32[768]{0:T(1024)}, f32[768]{0:T(1024)S(1)}, u32[]{:S(2)}) copy-start(f32[768]{0:T(1024)S(1)} %get-tuple-element.77) | copy-start | bytes 9220
  24.1 100.5 %copy-start.168 = (f32[768]{0:T(1024)}, f32[768]{0:T(1024)S(1)}, u32[]{:S(2)}) copy-start(f32[768]{0:T(1024)S(1)} %get-tuple-element.76) | copy-start | bytes 9220
  24.2 187.2 %copy-start.117 = (f32[768]{0:T(1024)}, f32[768]{0:T(1024)S(1)}, u32[]{:S(2)}) copy-start(f32[768]{0:T(1024)S(1)} %get-tuple-element.74) | copy-start | bytes 9220
  49.4 159.1 %all-reduce.16.cloned.1.call-start = ((), (), s32[]{:S(2)}) async-start(), calls=%async_computation.11 | async-start | bytes 6291456 | tf_op jit(solution)/shard_map/psum | solution.py:248
  139.7 154.9 %all-reduce.18.cloned.1.call-start = ((), (), s32[]{:S(2)}) async-start(), calls=%async_computation.12 | async-start | bytes 6291456 | tf_op jit(solution)/shard_map/psum | solution.py:247
  140.2 178.6 %copy-start.128 = (f32[3,64]{1,0:T(4,128)}, f32[3,64]{1,0:T(4,128)S(1)}, u32[]{:S(2)}) copy-start(f32[3,64]{1,0:T(4,128)S(1)} %add.645) | copy-start | bytes 2308
  140.3 179.1 %copy-start.100 = (f32[3,64]{1,0:T(4,128)}, f32[3,64]{1,0:T(4,128)S(1)}, u32[]{:S(2)}) copy-start(f32[3,64]{1,0:T(4,128)S(1)} %add.654) | copy-start | bytes 2308
  140.5 80.1 %copy-start.94 = (f32[3,64]{1,0:T(4,128)}, f32[3,64]{1,0:T(4,128)S(1)}, u32[]{:S(2)}) copy-start(f32[3,64]{1,0:T(4,128)S(1)} %add.637) | copy-start | bytes 2308
  226.0 161.1 %all-reduce.20.cloned.1.call-start = ((), (), s32[]{:S(2)}) async-start(), calls=%async_computation.13 | async-start | bytes 6291456 | tf_op jit(solution)/shard_map/psum | solution.py:268
  318.3 179.3 %all-reduce.22.cloned.1.call-start = ((), (), s32[]{:S(2)}) async-start(), calls=%async_computation.14 | async-start | bytes 6291456 | tf_op jit(solution)/shard_map/psum | solution.py:269
  428.9 154.0 %all-reduce.24.cloned.1.call-start = ((), (), s32[]{:S(2)}) async-start(), calls=%async_computation.15 | async-start | bytes 6291456 | tf_op jit(solution)/shard_map/psum | solution.py:268
  514.3 225.1 %all-reduce.26.cloned.1.call-start = ((), (), s32[]{:S(2)}) async-start(), calls=%async_computation.26 | async-start | bytes 12582912 | tf_op jit(solution)/shard_map/psum | solution.py:248
  619.3 186.1 %reduce-scatter.39.cloned.1.call-start = ((), (), s32[]{:S(2)}) async-start(), calls=%async_computation.23 | async-start | bytes 884736
  623.3 251.9 %reduce-scatter.35.cloned.1.call-start = ((), (), s32[]{:S(2)}) async-start(), calls=%async_computation.21 | async-start | bytes 2211840
  638.0 301.7 %reduce-scatter.37.cloned.1.call-start = ((), (), s32[]{:S(2)}) async-start(), calls=%async_computation.22 | async-start | bytes 884736
  641.6 370.2 %reduce-scatter.31.cloned.1.call-start = ((), (), s32[]{:S(2)}) async-start(), calls=%async_computation.19 | async-start | bytes 2654208 | tf_op jit(solution)/shard_map/reduce_scatter | solution.py:275
  646.6 437.1 %reduce-scatter.29.cloned.1.call-start = ((), (), s32[]{:S(2)}) async-start(), calls=%async_computation.18 | async-start | bytes 2654208 | tf_op jit(solution)/shard_map/reduce_scatter | solution.py:275
  651.9 503.9 %reduce-scatter.27.cloned.1.call-start = ((), (), s32[]{:S(2)}) async-start(), calls=%async_computation.17 | async-start | bytes 2654208 | tf_op jit(solution)/shard_map/reduce_scatter | solution.py:274
  657.6 81.8 %copy-start.90 = (f32[1024]{0:T(1024)S(1)}, f32[1024]{0:T(1024)}, u32[]{:S(2)}) copy-start(f32[1024]{0:T(1024)} %copy-done.89) | copy-start | bytes 12292
  657.6 81.8 %copy-start.104 = (pred[1024]{0:T(1024)(128)(4,1)S(1)}, pred[1024]{0:T(1024)(128)(4,1)}, u32[]{:S(2)}) copy-start(pred[1024]{0:T(1024)(128)(4,1)} %copy-done.103) | copy-start | bytes 3076
  657.6 81.8 %copy-start.121 = (f32[1024]{0:T(1024)S(1)}, f32[1024]{0:T(1024)}, u32[]{:S(2)}) copy-start(f32[1024]{0:T(1024)} %copy-done.120) | copy-start | bytes 12292
  657.6 81.7 %copy-start.123 = (f32[768]{0:T(1024)S(1)}, f32[768]{0:T(1024)}, u32[]{:S(2)}) copy-start(f32[768]{0:T(1024)} %copy-done.122) | copy-start | bytes 9220
  657.6 570.4 %reduce-scatter.25.cloned.1.call-start = ((), (), s32[]{:S(2)}) async-start(), calls=%async_computation.16 | async-start | bytes 2654208 | tf_op jit(solution)/shard_map/reduce_scatter | solution.py:274
  662.4 77.0 %copy-start.10 = (bf16[1024,768]{1,0:T(8,128)(2,1)S(1)}, bf16[1024,768]{1,0:T(8,128)(2,1)}, u32[]{:S(2)}) copy-start(bf16[1024,768]{1,0:T(8,128)(2,1)} %copy-done.9) | copy-start | bytes 4718596
  662.4 629.5 %reduce-scatter.41.cloned.1.call-start = ((), (), s32[]{:S(2)}) async-start(), calls=%async_computation.24 | async-start | bytes 442368
  744.4 612.0 %reduce-scatter.43.cloned.1.call-start = ((), (), s32[]{:S(2)}) async-start(), calls=%async_computation.25 | async-start | bytes 442368
  745.6 680.3 %reduce-scatter.33.cloned.1.call-start = ((), (), s32[]{:S(2)}) async-start(), calls=%async_computation.20 | async-start | bytes 2211840
  754.5 186.9 %copy-start.142 = (f32[768]{0:T(1024)S(1)}, f32[768]{0:T(1024)}, u32[]{:S(2)}) copy-start(f32[768]{0:T(1024)} %get-tuple-element.70) | copy-start | bytes 9220
  953.8 474.5 %copy-start.1 = (bf16[1024,768]{1,0:T(8,128)(2,1)S(1)}, bf16[1024,768]{1,0:T(8,128)(2,1)}, u32[]{:S(2)}) copy-start(bf16[1024,768]{1,0:T(8,128)(2,1)} %param.11) | copy-start | bytes 4718596
  (175 other events, 1743.8 us)
Sparse Core Ops, SparseCore 0:
  49.5 71.1 all-reduce.13
  139.9 68.5 all-reduce.15
  226.1 68.5 all-reduce.17
  318.5 68.5 all-reduce.19
  429.0 68.5 all-reduce.21
  514.4 68.5 all-reduce.23
  619.4 119.8 all-reduce.25
  742.7 62.7 reduce-scatter.38
  809.3 65.8 reduce-scatter.34
  878.4 61.3 reduce-scatter.36
  943.7 68.0 reduce-scatter.30
  1015.5 68.0 reduce-scatter.28
  1087.6 68.2 reduce-scatter.26
  1159.6 68.3 reduce-scatter.24
  1231.5 60.4 reduce-scatter.40
  1296.0 60.3 reduce-scatter.42
  1360.1 65.7 reduce-scatter.32
where the time goes:
time: 1440 us
  waiting for transfers between devices  1080 us (75%)
  matrix products  132 us (9%)
  other arithmetic  91.7 us (6%)
  local copies, waits for them, and re-layouts  70.4 us (5%)
  blocking collectives  35.4 us (2%)
  between operations  18 us (1%)
    psum x7, waiting for transfers between devices, body(): lax.psum(partial_value, 'mp')  480 us
    unnamed x23, waiting for transfers between devices  337 us
    reduce_scatter x2, waiting for transfers between devices, body(): lax.psum_scatter(grads[2], 'dp', scatter_dimension=0, tiled=True)  142 us
    reduce_scatter x2, waiting for transfers between devices, body(): lax.psum_scatter(grads[3], 'dp', scatter_dimension=1, tiled=True)  126 us
    unnamed x398, local copies, waits for them, and re-layouts  47.3 us
    unnamed x1, blocking collectives  35.4 us
  transfers between devices with their start and end apart: 17, of which 17 were waited for; matrix products, arithmetic and copies ran while one was open for 7% of the time, Pallas kernels for 0%

commit v1 on v0

v1 whole, which is shorter than its diff:
```python
import math

import jax
import jax.numpy as jnp
from jax import lax
from jax.experimental import pallas as pl
from jax.experimental.pallas import tpu as pltpu
from jax.sharding import PartitionSpec as P

MESH = pl.DeviceIdType.MESH
F32, BF16 = jnp.float32, jnp.bfloat16
HEAD = 64
LANES = 128
EPS = 1e-6
SCALE = HEAD**-0.5
EXP2_SCALE = SCALE / math.log(2.0)
CHUNK = 256
HALF = CHUNK // 2
WINDOW = 3
IMAGES = 8
EMPTY = HEAD + IMAGES
PAD = EMPTY + 1
APART = 2048.0
ROW_VECTORS, HEAD_VECTORS = 6, 6
UP_BIAS_ROW, HEAD_ROW, VEC_ROWS = 8, 9, 16


def mm(left, right):
    return jnp.dot(left, right, preferred_element_type=F32)


def mt(left, right):
    return lax.dot_general(left, right, (((1,), (1,)), ((), ())), preferred_element_type=F32)


def tm(left, right):
    return lax.dot_general(left, right, (((0,), (0,)), ((), ())), preferred_element_type=F32)


def norm_rows(values):
    center = values - jnp.mean(values, axis=-1, keepdims=True)
    rstd = lax.rsqrt(jnp.mean(center * center, axis=-1, keepdims=True) + EPS)
    return center * rstd, rstd


def norm_back(grad, hat, rstd):
    mean_grad = jnp.mean(grad, axis=-1, keepdims=True)
    mean_cross = jnp.mean(grad * hat, axis=-1, keepdims=True)
    return rstd * (grad - mean_grad - hat * mean_cross)


def head_mean(values):
    return jnp.sum(values, axis=-1, keepdims=True) * (1.0 / HEAD)


def norm_head(values, real):
    center = (values - head_mean(values)) * real
    rstd = lax.rsqrt(head_mean(center * center) + EPS)
    return center * rstd, rstd


def norm_head_back(grad, hat, rstd, real):
    return (rstd * real) * (grad - head_mean(grad) - hat * head_mean(grad * hat))


def column_sum(values):
    return jnp.sum(values, axis=0, keepdims=True)


def bit_of(index, bit):
    return (index // (1 << bit)) % 2


def flipped(index, bits):
    for bit in bits:
        index = index + (1 << bit) * (1 - 2 * bit_of(index, bit))
    return index


class GradSum:
    def __init__(self, n_dp, me, mp, order, grad, landing, send_sem, recv_sem, credit, first, out, out_sem):
        self.me, self.mp, self.order = me, mp, order
        self.steps = len(order)
        self.counts = [n_dp >> (k + 1) for k in range(self.steps)]
        self.offsets = [sum(self.counts[:k]) for k in range(self.steps)]
        self.grad, self.landing = grad, landing
        self.send_sem, self.recv_sem, self.credit = send_sem, recv_sem, credit
        self.first, self.out, self.out_sem = first, out, out_sem
        self.opened = set()
        self.taken = [0] * self.steps

    def turn(self, k):
        return sorted(range(self.counts[k]), key=lambda m: (m % 2 == 0, -m))

    def events(self):
        found = [(k, m) for k in range(self.steps) for m in self.turn(k)]
        if self.steps == 3:
            found = [(0, 3), (0, 1), (0, 2), (1, 1), (0, 0), (1, 0), (2, 0)]
        return found

    def later_bits(self, k, m):
        return [self.order[k + 1 + t] for t in range(self.steps - k - 1) if (m >> t) & 1]

    def copy(self, k, m):
        slot = self.offsets[k] + m
        block = flipped(self.me, [self.order[k]] + self.later_bits(k, m))
        return pltpu.make_async_remote_copy(
            src_ref=self.grad.at[block],
            dst_ref=self.landing.at[slot],
            send_sem=self.send_sem.at[slot],
            recv_sem=self.recv_sem.at[slot],
            device_id=(flipped(self.me, [self.order[k]]), self.mp),
            device_id_type=MESH,
        )

    def send(self, k, m):
        if not self.first and k not in self.opened:
            pl.semaphore_wait(self.credit.at[k], 1)
        self.opened.add(k)
        self.copy(k, m).start()

    def start(self):
        for m in self.turn(0):
            self.send(0, m)

    def result(self):
        return pltpu.make_async_copy(self.grad.at[self.me], self.out, self.out_sem)

    def take(self, k, m):
        self.copy(k, m).wait()
        block = flipped(self.me, self.later_bits(k, m))
        self.grad[block] += self.landing[self.offsets[k] + m]
        if k + 1 < self.steps and m % 2 == 1:
            self.send(k + 1, m // 2)
        self.taken[k] += 1
        if self.first and self.taken[k] == self.counts[k]:
            pl.semaphore_signal(
                self.credit.at[k], inc=1, device_id=(flipped(self.me, [self.order[k]]), self.mp), device_id_type=MESH
            )
        if sum(self.taken) == sum(self.counts):
            self.result().start()


def spread(grad_sum, places, plan):
    events = grad_sum.events()
    for position, event in enumerate(events):
        place = places[position * len(places) // len(events)]
        plan.setdefault(place, []).append((grad_sum, event))


def make_kernel(n_dp, tokens, width, hidden, heads, layers):
    chunks = tokens // CHUNK
    bits = n_dp.bit_length() - 1
    block = width // n_dp
    slots = heads * LANES
    qkv_cols = 3 * heads * HEAD
    last = layers - 1

    def kernel(
        keep_ref,
        seg_ref,
        hv_ref,
        ub_ref,
        rv_ref,
        patches_in,
        cot_in,
        wq_in,
        wo_in,
        wu_in,
        wd_in,
        packed_out,
        gpatch_out,
        gm_out,
        ga_out,
        vec_out,
        spill_q,
        spill_k,
        spill_v,
        spill_o,
        spill_a,
        spill_y,
        INP,
        WQ,
        WO,
        WU,
        WD,
        X,
        X1,
        A,
        C0,
        CT,
        Q,
        K,
        V,
        O,
        LSE,
        G0,
        GP0,
        QA,
        KA,
        LIVE,
        TROW,
        TCOL,
        PART,
        DBUF,
        YBUF,
        CBUF,
        CSEND,
        DX,
        DQ,
        DK,
        DV,
        GM,
        GA,
        RM,
        RA,
        VEC,
        VLAND,
        STAGE,
        load_sem,
        spill_sem,
        stage_sem,
        d_send,
        d_recv,
        y_send,
        y_recv,
        c_send,
        c_recv,
        m_send,
        m_recv,
        a_send,
        a_recv,
        credit_m,
        credit_a,
        v_send,
        v_recv,
        out_sem,
    ):
        dp = lax.axis_index("dp")
        mp = lax.axis_index("mp")
        core = mp % 2
        sibling = mp + 1 - 2 * core
        across = (mp + 2) % 4

        barrier = pltpu.get_barrier_semaphore()
        for other in (sibling, across):
            pl.semaphore_signal(barrier, inc=1, device_id=(dp, other), device_id_type=MESH)
        for bit in range(bits):
            pl.semaphore_signal(barrier, inc=1, device_id=(flipped(dp, [bit]), mp), device_id_type=MESH)

        lane = lax.broadcasted_iota(jnp.int32, (1, LANES), 1)
        real = (lane < HEAD).astype(F32)

        def load(source, target, index):
            return pltpu.make_async_copy(source, target, load_sem.at[index])

        def load_attn(layer):
            return [load(wq_in.at[layer], WQ, 0), load(wo_in.at[layer], WO, 1)]

        def load_mlp(layer):
            return [load(wu_in.at[layer], WU, 2), load(wd_in.at[layer], WD, 3)]

        def spills(back):
            pairs = [(Q, spill_q), (K, spill_k), (V, spill_v), (O, spill_o), (A, spill_a)]
            return [
                pltpu.make_async_copy(*((far, near) if back else (near, far)), spill_sem.at[index])
                for index, (near, far) in enumerate(pairs)
            ]

        def start(copies):
            for copy in copies:
                copy.start()

        def wait(copies):
            for copy in copies:
                copy.wait()

        def to_sibling(chunk):
            slot = chunk % 2
            return pltpu.make_async_remote_copy(
                src_ref=PART.at[chunk, 1 - core],
                dst_ref=DBUF.at[slot],
                send_sem=d_send.at[slot],
                recv_sem=d_recv.at[slot],
                device_id=(dp, sibling),
                device_id_type=MESH,
            )

        def to_across(phase, chunk):
            slot = phase % 2
            return pltpu.make_async_remote_copy(
                src_ref=PART.at[chunk, core],
                dst_ref=YBUF.at[slot, chunk],
                send_sem=y_send.at[slot, chunk],
                recv_sem=y_recv.at[slot, chunk],
                device_id=(dp, across),
                device_id_type=MESH,
            )

        def to_gather(chunk):
            slot = chunk % 2
            return pltpu.make_async_remote_copy(
                src_ref=CSEND,
                dst_ref=CBUF.at[slot],
                send_sem=c_send.at[slot],
                recv_sem=c_recv.at[slot],
                device_id=(dp, sibling),
                device_id_type=MESH,
            )

        def put_part(chunk, values):
            PART[chunk] = values.reshape(2, HALF, width)

        def send_part(phase, chunk):
            copy = to_sibling(chunk)
            copy.start()
            copy.wait()
            PART[chunk, core] += DBUF[chunk % 2]
            to_across(phase, chunk).start()

        def total_of(phase, chunk):
            to_across(phase, chunk).wait()
            return PART[chunk, core] + YBUF[phase % 2, chunk]

        def gather(chunk, own, target):
            CSEND[...] = own
            copy = to_gather(chunk)
            copy.start()
            target[core] = own.astype(target.dtype)
            copy.wait()
            target[1 - core] = CBUF[chunk % 2].astype(target.dtype)

        def whole(ref, chunk):
            return ref[chunk].reshape(CHUNK, width)

        def add_vec(layer, row, values):
            VEC[layer, row : row + 1, 0 : values.shape[1]] += values

        def rv(layer, row):
            return rv_ref[layer, row : row + 1, :]

        def hv(layer, row, head):
            return hv_ref[layer, row : row + 1, head * LANES : (head + 1) * LANES]

        def head_cols(values, head, first=0):
            return values[:, first + head * LANES : first + (head + 1) * LANES]

        def pack(chunk):
            rows = lax.broadcasted_iota(jnp.int32, (CHUNK, tokens), 0) + chunk * CHUNK
            chosen = (TROW[0:1, :].astype(jnp.int32) == rows).astype(F32).astype(BF16)
            values = mm(chosen, INP[...])
            classes = mm(chosen, QA[...].reshape(tokens, LANES))
            alive = jnp.sum(classes, axis=-1, keepdims=True)
            LIVE[chunk] = jnp.broadcast_to(alive, (CHUNK, LANES))
            KA[chunk] = (classes + jnp.where(lane == EMPTY, 1.0 - alive, 0.0)).astype(BF16)
            put_part(chunk, values)
            X[0, chunk] = PART[chunk, core]
            hat, _ = norm_rows(values)
            A[chunk] = (hat * (1.0 + rv(0, 0)) + rv(0, 1)).astype(BF16).reshape(2, HALF, width)

        def apart_of(chunk):
            is_class = (lane >= HEAD) & (lane <= PAD)
            return jnp.where(is_class, -APART * (1.0 - KA[chunk].astype(F32)), 0.0)

        def project(layer, chunk):
            raw = mm(whole(A, chunk), WQ[...])
            apart = apart_of(chunk)
            classes = KA[chunk].astype(F32)
            ones = (lane == HEAD).astype(F32)
            for head in range(heads):
                hat, _ = norm_head(head_cols(raw, head) + hv(layer, 0, head), real)
                Q[head, chunk] = (
                    (hat * (1.0 + hv(layer, 3, head)) + hv(layer, 5, head)).astype(BF16) + apart.astype(BF16)
                )
                hat, _ = norm_head(head_cols(raw, head, slots) + hv(layer, 1, head), real)
                K[head, chunk + 1] = (hat * (1.0 + hv(layer, 4, head))).astype(BF16) + classes.astype(BF16)
                V[head, chunk + 1] = (head_cols(raw, head, 2 * slots) + hv(layer, 2, head) + ones).astype(BF16)

        def window(ref, head, chunk):
            return ref[head, pl.ds(chunk, WINDOW)].reshape(WINDOW * CHUNK, LANES)

        def attend(layer, chunk):
            for head in range(heads):
                keys, values = window(K, head, chunk), window(V, head, chunk)
                scores = mt(keys, Q[head, chunk])
                expo = jnp.exp2(scores * EXP2_SCALE).astype(BF16)
                out = tm(values, expo)
                total = out[HEAD : HEAD + 1, :]
                LSE[layer, head, chunk] = jnp.log(total) * (1.0 / math.log(2.0))
                out = (out * (1.0 / total)).T
                O[head, chunk] = jnp.where(lane < HEAD, out, 0.0).astype(BF16)
            joined = jnp.concatenate([O[head, chunk] for head in range(heads)], axis=1)
            put_part(chunk, mm(joined, WO[...]))

        def attn_forward(layer, phase):
            def slot(i, carry):
                @pl.when(i < chunks)
                def _():
                    if layer == 0:
                        pack(i)
                    else:
                        x = X1[layer - 1, i] + total_of(phase - 1, i) + rv(layer - 1, 5)
                        X[layer, i] = x
                        hat, _ = norm_rows(x)
                        own = (hat * (1.0 + rv(layer, 0)) + rv(layer, 1)).astype(BF16).astype(F32)
                        gather(i, own, A.at[i])
                    project(layer, i)

                @pl.when(i > 0)
                def _():
                    attend(layer, i - 1)
                    send_part(phase, i - 1)

                return carry

            lax.fori_loop(0, chunks + 1, slot, 0)

        def middle(layer, phase, chunk, target):
            x1 = X[layer, chunk] + total_of(phase - 1, chunk) + rv(layer, 4)
            X1[layer, chunk] = x1
            hat, _ = norm_rows(x1)
            own = (hat * (1.0 + rv(layer, 2)) + rv(layer, 3)).astype(BF16).astype(F32)
            gather(chunk, own, target)

        def up(layer, second):
            before = mm(second, WU[...]) + ub_ref[layer : layer + 1, :]
            cdf = 0.5 * (1.0 + lax.erf(before * math.sqrt(0.5)))
            density = jnp.exp(before * before * -0.5) * (1.0 / math.sqrt(2.0 * math.pi))
            return (before * cdf).astype(BF16), cdf + before * density

        def mlp_forward(layer, phase):
            def slot(i, carry):
                middle(layer, phase, i, C0.at[i])
                act, slope = up(layer, whole(C0, i))
                G0[i] = act
                GP0[i] = slope.astype(BF16)
                put_part(i, mm(act, WD[...]))
                send_part(phase, i)
                return carry

            lax.fori_loop(0, chunks, slot, 0)

        def mlp_grads(layer, second, act, grad_out, grad_before):
            GM[layer, :, :, 0:hidden] += tm(second, grad_before).reshape(n_dp, block, hidden)
            GM[layer, :, :, hidden:] += tm(grad_out, act).reshape(n_dp, block, hidden)
            add_vec(layer, UP_BIAS_ROW, column_sum(grad_before.astype(F32)))

        def pump(name, i):
            for (where, index), events in plan.items():
                if where == name:

                    @pl.when(i == index)
                    def _():
                        for grad_sum, event in events:
                            grad_sum.take(*event)

        def mlp_turn(layer, phase):
            GM[layer] = jnp.zeros((n_dp, block, 2 * hidden), F32)

            def slot(i, carry):
                middle(layer, phase, i, CT.at[0])
                second = whole(CT, 0)
                act, slope = up(layer, second)

                @pl.when(i > 0)
                def _():
                    pltpu.make_async_copy(STAGE.at[0], spill_y.at[i - 1], stage_sem.at[0]).wait()

                STAGE[0] = mm(act, WD[...]).reshape(2, HALF, width)
                pltpu.make_async_copy(STAGE.at[0], spill_y.at[i], stage_sem.at[0]).start()
                grad = INP[pl.ds(i * CHUNK, CHUNK), :].astype(F32) * LIVE[i, :, 0:1]
                CT[1] = grad.astype(BF16).reshape(2, HALF, width)
                own = CT[1, core].astype(F32)
                DX[i] = own
                add_vec(layer, 5, column_sum(own))
                grad = grad.astype(BF16)
                grad_before = (mt(grad, WD[...]) * slope).astype(BF16)
                put_part(i, mt(grad_before, WU[...]))
                send_part(phase, i)
                mlp_grads(layer, second, act, grad, grad_before)
                return carry

            lax.fori_loop(0, chunks, slot, 0)
            pltpu.make_async_copy(STAGE.at[0], spill_y.at[chunks - 1], stage_sem.at[0]).wait()

        def input_back(layer, phase, chunk):
            grad_normed = total_of(phase - 1, chunk)
            hat, rstd = norm_rows(X[layer, chunk])
            add_vec(layer, 0, column_sum(grad_normed * hat))
            add_vec(layer, 1, column_sum(grad_normed))
            return DX[chunk] + norm_back(grad_normed * (1.0 + rv(layer, 0)), hat, rstd)

        def mlp_backward(layer, phase, name):
            GM[layer] = jnp.zeros((n_dp, block, 2 * hidden), F32)

            def slot(i, carry):
                grad = input_back(layer + 1, phase, i)
                DX[i] = grad
                own = grad.astype(BF16).astype(F32)
                add_vec(layer, 5, column_sum(own))
                gather(i, own, CT.at[0])
                grad = whole(CT, 0)
                grad_before = (mt(grad, WD[...]) * GP0[i].astype(F32)).astype(BF16)
                put_part(i, mt(grad_before, WU[...]))
                send_part(phase, i)
                mlp_grads(layer, whole(C0, i), G0[i], grad, grad_before)
                pump(name, i)
                return carry

            lax.fori_loop(0, chunks, slot, 0)

        def attend_back(layer, chunk):
            grad = whole(CT, 0)
            grad_heads = mt(grad, WO[...]).astype(BF16)
            ring = chunk % WINDOW
            for head in range(heads):
                grad_o = head_cols(grad_heads, head)
                query = Q[head, chunk]
                keys, values = window(K, head, chunk), window(V, head, chunk)
                delta = column_sum((O[head, chunk].astype(F32) * grad_o.astype(F32)).T)
                probs = jnp.exp2(mt(keys, query) * EXP2_SCALE - LSE[layer, head, chunk])
                grad_scores = (probs * (mt(values, grad_o) - delta)).astype(BF16)
                grad_v = mm(probs.astype(BF16), grad_o)
                grad_k = mm(grad_scores, query)
                DQ[chunk % 2, head] = tm(grad_scores, keys) * SCALE
                for part in range(WINDOW):
                    place = (ring + part + WINDOW - 1) % WINDOW
                    rows = slice(part * CHUNK, (part + 1) * CHUNK)
                    if part < WINDOW - 1:
                        DV[head, place] += grad_v[rows]
                        DK[head, place] += grad_k[rows]
                    else:
                        DV[head, place] = grad_v[rows]
                        DK[head, place] = grad_k[rows]
            out = [O[head, chunk].astype(F32) for head in range(heads)]
            pairs = [pltpu.roll(out[0], HEAD, 1), out[1] + pltpu.roll(out[2], HEAD, 1)]
            packed = jnp.concatenate(pairs, axis=1).astype(BF16)
            GA[layer, :, :, qkv_cols - HEAD :] += tm(grad, packed).reshape(n_dp, block, 2 * LANES)

        def project_back(layer, chunk):
            normed = whole(A, chunk)
            raw = mm(normed, WQ[:, 0 : 2 * slots])
            ring, turn = chunk % WINDOW, chunk % 2
            parts = [None] * (3 * heads)
            for head in range(heads):
                cols = head * LANES
                for kind, grad in ((0, DQ[turn, head]), (1, DK[head, ring] * SCALE)):
                    hat, rstd = norm_head(head_cols(raw, head, kind * slots) + hv(layer, kind, head), real)
                    gain = (1.0 + hv(layer, 3 + kind, head)) * real
                    inner = norm_head_back(grad * gain, hat, rstd, real)
                    sums = [(HEAD_ROW + kind, inner), (HEAD_ROW + 3 + kind, grad * hat)]
                    if kind == 0:
                        sums.append((HEAD_ROW + 5, grad))
                    for row, values in sums:
                        VEC[layer, row : row + 1, cols : cols + LANES] += column_sum(values)
                    parts[kind * heads + head] = inner
                grad_v = DV[head, ring]
                VEC[layer, HEAD_ROW + 2 : HEAD_ROW + 3, cols : cols + LANES] += column_sum(grad_v)
                parts[2 * heads + head] = grad_v
            padded = jnp.concatenate([part.astype(BF16) for part in parts], axis=1)
            put_part(chunk, mt(padded, WQ[...]))
            pairs = []
            for first in range(0, len(parts), 2):
                if first + 1 < len(parts):
                    pairs.append(parts[first] + pltpu.roll(parts[first + 1], HEAD, 1))
                else:
                    pairs.append(parts[first])
            dense = jnp.concatenate([pair.astype(BF16) for pair in pairs], axis=1)
            cols = len(pairs) * LANES
            GA[layer, :, :, 0:cols] += tm(normed, dense).reshape(n_dp, block, cols)

        def attn_backward(layer, phase, name):
            GA[layer] = jnp.zeros((n_dp, block, qkv_cols + heads * HEAD), F32)
            DK[...] = jnp.zeros_like(DK)
            DV[...] = jnp.zeros_like(DV)

            def slot(i, carry):
                @pl.when(i < chunks)
                def _():
                    grad_second = total_of(phase - 1, i)
                    hat, rstd = norm_rows(X1[layer, i])
                    add_vec(layer, 2, column_sum(grad_second * hat))
                    add_vec(layer, 3, column_sum(grad_second))
                    grad = DX[i] + norm_back(grad_second * (1.0 + rv(layer, 2)), hat, rstd)
                    DX[i] = grad
                    own = grad.astype(BF16).astype(F32)
                    add_vec(layer, 4, column_sum(own))
                    gather(i, own, CT.at[0])
                    attend_back(layer, i)

                @pl.when(i > 0)
                def _():
                    project_back(layer, i - 1)
                    send_part(phase, i - 1)

                pump(name, i)
                return carry

            lax.fori_loop(0, chunks + 1, slot, 0)

        near_first = [1, 0] + list(range(2, bits)) if bits > 1 else list(range(bits))

        def grad_sum(kind, layer):
            if kind == 0:
                parts = (list(range(bits)), GM, RM, m_send, m_recv, credit_m, gm_out)
            else:
                parts = (near_first, GA, RA, a_send, a_recv, credit_a, ga_out)
            order, grad, landing, sends, recvs, credit, out = parts
            return GradSum(
                n_dp, dp, mp, order, grad.at[layer], landing, sends, recvs, credit, layer == last,
                out.at[layer], out_sem.at[2 * layer + kind],
            )

        mlp_last, attn_last = grad_sum(0, last), grad_sum(1, last)
        mlp_first, attn_first = grad_sum(0, 0), grad_sum(1, 0)
        plan = {}
        spread(mlp_last, [("a1", 2), ("a1", 3), ("a1", 4), ("m0", 0), ("m0", 1), ("m0", 2), ("m0", 3)], plan)
        spread(attn_last, [("m0", 2), ("m0", 3), ("a0", 0), ("a0", 1), ("a0", 2)], plan)
        spread(mlp_first, [("a0", 3), ("a0", 4), ("end", 0), ("end", 1), ("end", 2), ("end", 3)], plan)

        first_loads = [load(patches_in, INP, 4)]
        start(first_loads + load_attn(0) + load_mlp(0))
        VEC[...] = jnp.zeros_like(VEC)
        keep = jnp.broadcast_to(keep_ref[...].astype(F32), (8, tokens))
        earlier = lax.broadcasted_iota(jnp.int32, (tokens, tokens), 0)
        later = lax.broadcasted_iota(jnp.int32, (tokens, tokens), 1)
        count = mm(keep.astype(BF16), (earlier <= later).astype(F32).astype(BF16))
        place = jnp.where(keep > 0.0, count - 1.0, 2.0 * tokens)
        TROW[...] = place
        TCOL[...] = jnp.broadcast_to(place[0:1, :], (LANES, tokens)).T
        segment = jnp.broadcast_to(seg_ref[...].astype(F32), (LANES, tokens)).T
        QA[...] = (segment.astype(jnp.int32) == lane - HEAD).astype(F32).astype(BF16).reshape(chunks, CHUNK, LANES)
        padding = jnp.broadcast_to((lane == PAD).astype(F32), (CHUNK, LANES)).astype(BF16)
        for head in range(heads):
            for edge in (0, chunks + 1):
                K[head, edge] = padding
                V[head, edge] = jnp.zeros((CHUNK, LANES), BF16)
        wait(first_loads + load_attn(0))
        pl.semaphore_wait(barrier, 2 + bits)

        attn_forward(0, 0)
        cot_load = [load(cot_in, INP, 4)]
        start(spills(False) + load_attn(1) + cot_load)
        wait(load_mlp(0))
        mlp_forward(0, 1)
        wait(spills(False) + load_attn(1))
        start(load_mlp(1))
        attn_forward(1, 2)
        wait(load_mlp(1) + cot_load)
        mlp_turn(1, 3)
        start(load_mlp(0))
        mlp_last.start()
        attn_backward(1, 4, "a1")
        attn_last.start()
        start(spills(True) + load_attn(0))
        wait(load_mlp(0))
        mlp_backward(0, 5, "m0")
        mlp_first.start()
        wait(spills(True) + load_attn(0))
        attn_backward(0, 6, "a0")
        attn_first.start()

        def end_slot(i, carry):
            rows = input_back(0, 7, i)
            reload = pltpu.make_async_copy(spill_y.at[i], PART.at[i], stage_sem.at[0])
            reload.start()
            CSEND[...] = rows
            copy = to_gather(i)
            copy.start()
            X1[0, i] = rows
            copy.wait()
            X[last, i] = CBUF[i % 2]
            reload.wait()
            send_part(7, i)
            pump("end", i)
            return carry

        lax.fori_loop(0, chunks, end_slot, 0)

        def vec_copy(step, target):
            return pltpu.make_async_remote_copy(
                src_ref=VEC,
                dst_ref=VLAND.at[step],
                send_sem=v_send.at[step],
                recv_sem=v_recv.at[step],
                device_id=target,
                device_id_type=MESH,
            )

        copy = vec_copy(0, (dp, sibling))
        copy.start()
        copy.wait()
        VEC[:, 0:UP_BIAS_ROW, :] += VLAND[0, :, 0:UP_BIAS_ROW, :]

        def unpack(patch_chunk, stage):
            stage[...] = jnp.zeros(stage.shape, F32)
            place = TCOL[pl.ds(patch_chunk * CHUNK, CHUNK), 0:1].astype(jnp.int32)

            def add_slots(chunk, carry):
                slot = lax.broadcasted_iota(jnp.int32, (CHUNK, CHUNK), 1) + chunk * CHUNK
                chosen = (place == slot).astype(F32).astype(BF16)
                own, other = X1[0, chunk], X[last, chunk]
                rest = jnp.concatenate([jnp.where(core == 0, own, other), jnp.where(core == 0, other, own)], axis=0)
                for _ in range(3):
                    piece = rest.astype(BF16)
                    stage[...] += mm(chosen, piece).reshape(stage.shape)
                    rest = rest - piece.astype(F32)
                return carry

            lax.fori_loop(0, patch_chunk + 1, add_slots, 0)

        def patch_copy(patch_chunk, turn):
            return pltpu.make_async_copy(STAGE.at[turn], gpatch_out.at[patch_chunk], stage_sem.at[turn])

        for patch_chunk in range(chunks):
            turn = patch_chunk % 2
            if patch_chunk >= 2:
                patch_copy(patch_chunk - 2, turn).wait()
            unpack(patch_chunk, STAGE.at[turn])
            patch_copy(patch_chunk, turn).start()
            if patch_chunk < bits:
                copy = vec_copy(1 + patch_chunk, (flipped(dp, [patch_chunk]), mp))
                copy.start()
                copy.wait()
                VEC[...] += VLAND[1 + patch_chunk]
        for step in range(chunks, bits):
            copy = vec_copy(1 + step, (flipped(dp, [step]), mp))
            copy.start()
            copy.wait()
            VEC[...] += VLAND[1 + step]
        vec_done = pltpu.make_async_copy(VEC, vec_out, out_sem.at[2 * layers])
        vec_done.start()
        for patch_chunk in range(max(0, chunks - 2), chunks):
            patch_copy(patch_chunk, patch_chunk % 2).wait()

        events = attn_first.events()

        def out_copy(chunk):
            return pltpu.make_async_copy(A.at[chunk], packed_out.at[chunk], spill_sem.at[0])

        def out_slot(i, carry):
            rows = (X1[last, i] + total_of(7, i) + rv(last, 5)) * LIVE[i, pl.ds(core * HALF, HALF), 0:1]
            gather(i, rows.astype(BF16).astype(F32), A.at[i])
            out_copy(i).start()
            return carry

        lax.fori_loop(0, chunks, out_slot, 0)
        for event in events:
            attn_first.take(*event)

        def out_wait(i, carry):
            out_copy(i).wait()
            return carry

        lax.fori_loop(0, chunks, out_wait, 0)
        vec_done.wait()
        for finished in (mlp_last, attn_last, mlp_first, attn_first):
            assert finished.taken == finished.counts
            finished.result().wait()

    return kernel


def body(n_dp, patches, patch_keep, patch_segment, cotangent, w_qkv, w_out, w_up, w_down, head_vectors, up_bias, row_vectors):
    tokens, width = patches.shape
    layers = w_qkv.shape[0]
    channels = w_qkv.shape[3]
    heads = channels // HEAD
    hidden = w_up.shape[2]
    chunks = tokens // CHUNK
    slots = heads * LANES
    bits = n_dp.bit_length() - 1
    block = width // n_dp
    attn_cols = 4 * channels

    def padded(values, axis):
        shape = values.shape
        split = values.reshape(shape[:axis] + (heads, HEAD) + shape[axis + 1 :])
        pads = [(0, 0)] * split.ndim
        pads[axis + 1] = (0, LANES - HEAD)
        return jnp.pad(split, pads).reshape(shape[:axis] + (slots,) + shape[axis + 1 :])

    wq = padded(w_qkv, 3).transpose(0, 2, 1, 3).reshape(layers, width, 3 * slots)
    wo = padded(w_out, 1)
    hv = padded(head_vectors, 2)
    any_space = pl.BlockSpec(memory_space=pl.ANY)
    vmem = pl.BlockSpec(memory_space=pltpu.VMEM)
    sds = jax.ShapeDtypeStruct
    half = (HALF, width)
    head_chunks = (heads, chunks, CHUNK, LANES)
    head_window = (heads, chunks + 2, CHUNK, LANES)
    out_shape = [
        sds((chunks, 2) + half, BF16),
        sds((chunks, 2) + half, F32),
        sds((layers, block, 2 * hidden), F32),
        sds((layers, block, attn_cols), F32),
        sds((layers, VEC_ROWS, width), F32),
        sds(head_chunks, BF16),
        sds(head_window, BF16),
        sds(head_window, BF16),
        sds(head_chunks, BF16),
        sds((chunks, 2) + half, BF16),
        sds((chunks, 2) + half, F32),
    ]
    v = pltpu.VMEM
    dma = pltpu.SemaphoreType.DMA
    scratch = [
        v((tokens, width), BF16),
        v((width, 3 * slots), BF16),
        v((slots, width), BF16),
        v((width, hidden), BF16),
        v((hidden, width), BF16),
        v((layers, chunks) + half, F32),
        v((layers, chunks) + half, F32),
        v((chunks, 2) + half, BF16),
        v((chunks, 2) + half, BF16),
        v((2, 2) + half, BF16),
        v(head_chunks, BF16),
        v(head_window, BF16),
        v(head_window, BF16),
        v(head_chunks, BF16),
        v((layers, heads, chunks, 1, CHUNK), F32),
        v((chunks, CHUNK, hidden), BF16),
        v((chunks, CHUNK, hidden), BF16),
        v((chunks, CHUNK, LANES), BF16),
        v((chunks, CHUNK, LANES), BF16),
        v((chunks, CHUNK, LANES), F32),
        v((8, tokens), F32),
        v((tokens, LANES), F32),
        v((chunks, 2) + half, F32),
        v((2,) + half, F32),
        v((2, chunks) + half, F32),
        v((2,) + half, F32),
        v(half, F32),
        v((chunks,) + half, F32),
        v((2, heads, CHUNK, LANES), F32),
        v((heads, WINDOW, CHUNK, LANES), F32),
        v((heads, WINDOW, CHUNK, LANES), F32),
        v((layers, n_dp, block, 2 * hidden), F32),
        v((layers, n_dp, block, attn_cols), F32),
        v((n_dp - 1, block, 2 * hidden), F32),
        v((n_dp - 1, block, attn_cols), F32),
        v((layers, VEC_ROWS, width), F32),
        v((bits + 1, layers, VEC_ROWS, width), F32),
        v((2, 2) + half, F32),
        dma((5,)),
        dma((5,)),
        dma((2,)),
        dma((2,)),
        dma((2,)),
        dma((2, chunks)),
        dma((2, chunks)),
        dma((2,)),
        dma((2,)),
        dma((n_dp - 1,)),
        dma((n_dp - 1,)),
        dma((n_dp - 1,)),
        dma((n_dp - 1,)),
        pltpu.SemaphoreType.REGULAR((bits,)),
        pltpu.SemaphoreType.REGULAR((bits,)),
        dma((bits + 1,)),
        dma((bits + 1,)),
        dma((2 * layers + 1,)),
    ]
    results = pl.pallas_call(
        make_kernel(n_dp, tokens, width, hidden, heads, layers),
        out_shape=out_shape,
        in_specs=[vmem] * 5 + [any_space] * 6,
        out_specs=[any_space] * len(out_shape),
        scratch_shapes=scratch,
        compiler_params=pltpu.CompilerParams(
            collective_id=0, has_side_effects=True, vmem_limit_bytes=64 * 2**20 - 2**16
        ),
    )(patch_keep, patch_segment, hv, up_bias, row_vectors, patches, cotangent, wq, wo, w_up, w_down)
    packed, grad_patches, gm, ga, vec = results[:5]

    place = lax.axis_index("dp")

    def mine(values):
        share = values.shape[-1] // n_dp
        return lax.dynamic_slice_in_dim(values, place * share, share, axis=values.ndim - 1)

    grad_qkv = ga[:, :, : 3 * channels].reshape(layers, block, 3, channels).transpose(0, 2, 1, 3)
    grad_out = ga[:, :, 3 * channels :].transpose(0, 2, 1)
    grad_up = gm[:, :, :hidden]
    grad_down = gm[:, :, hidden:].transpose(0, 2, 1)
    head_rows = vec[:, HEAD_ROW : HEAD_ROW + HEAD_VECTORS, :slots].reshape(layers, HEAD_VECTORS, heads, LANES)
    head_grads = mine(head_rows[..., :HEAD].reshape(layers, HEAD_VECTORS, channels))
    return (
        packed.reshape(tokens, width),
        grad_patches.reshape(tokens, width),
        grad_qkv,
        grad_out,
        grad_up,
        grad_down,
        head_grads,
        mine(vec[:, UP_BIAS_ROW, :hidden]),
        mine(vec[:, 0:ROW_VECTORS, :]),
    )


def solution(mesh):
    n_dp = mesh.shape["dp"]

    def step(*args):
        return body(n_dp, *args)

    return jax.shard_map(
        step,
        mesh=mesh,
        in_specs=(
            P("dp", None),
            P("dp", None),
            P("dp", None),
            P("dp", None),
            P(None, None, None, "mp"),
            P(None, "mp", None),
            P(None, None, "mp"),
            P(None, "mp", None),
            P(None, None, "mp"),
            P(None, "mp"),
            P(),
        ),
        out_specs=(
            P("dp", None),
            P("dp", None),
            P(None, None, "dp", "mp"),
            P(None, "mp", "dp"),
            P(None, "dp", "mp"),
            P(None, "mp", "dp"),
            P(None, None, ("mp", "dp")),
            P(None, ("mp", "dp")),
            P(None, None, "dp"),
        ),
        check_vma=False,
    )
```

time: 1440 us -> 382 us (0.27)
  waiting for transfers between devices: 1080 us -> 0 us
  Pallas kernels: 0 us -> 358 us
  matrix products: 132 us -> 0 us
  other arithmetic: 91.7 us -> 0 us
  local copies, waits for them, and re-layouts: 70.4 us -> 22.3 us
  blocking collectives: 35.4 us -> 0 us
  between operations: 18 us -> 0.72 us
    psum x7 -> x0, waiting for transfers between devices: 480 us -> none  [body(): lax.psum(partial_value, 'mp')]
    pallas_call x0 -> x1, Pallas kernels: none -> 358 us  [body(): pl.pallas_call(make_kernel(n_dp, tokens, width, hidden, heads, layers), o...]
    unnamed x23 -> x0, waiting for transfers between devices: 337 us -> none
    reduce_scatter x4 -> x0, waiting for transfers between devices: 268 us -> none  [the longest x2 142 us: body(): lax.psum_scatter(grads[2], 'dp', scatter_dimension=0, tiled=True)]
    dot_general x32 -> x0, matrix products: 122 us -> none  [the longest x4 20.2 us: contract_rows(): lax.dot_general(left, right, (((0,), (0,)), ((), ())), preferred_element_...]
    reduce_sum x28 -> x0, other arithmetic: 48.8 us -> none  [the longest x8 10.2 us: norm_rows(): center = values - jnp.mean(values, axis=-1, keepdims=True)]
    unnamed x398 -> x14, local copies, waits for them, and re-layouts: 47.3 us -> 8.01 us
    unnamed x1 -> x0, blocking collectives: 35.4 us -> none
  transfers between devices with their start and end apart: 17 -> 0, of which waited for: 17 -> 0; matrix products, arithmetic and copies ran while one was open for 7% -> 0% of each run, Pallas kernels for 0% -> 0%
where the time goes in v1:
time: 382 us; the launch traced here: 381 us
  Pallas kernels  358 us (94%)
  local copies, waits for them, and re-layouts  22.3 us (6%)
    pallas_call x1, Pallas kernels, body(): pl.pallas_call(make_kernel(n_dp, tokens, width, hidden, heads, layers), o...  358 us
    unnamed x14, local copies, waits for them, and re-layouts  8.01 us

profile of v1, /device:TPU:0, one launch (start us, length us, event | category | flops | bytes accessed | tf_op | source)
XLA Modules:
  0.0 381.0 jit_solution(17461016303367484910)
XLA Ops:
  0.6 0.8 reshape.55
  1.5 0.6 copy.27.hv_ref
  2.1 1.4 copy.28.rv_ref
  3.5 1.9 pad.13
  5.3 3.8 copy.29.wq_in
  9.2 2.2 pad.14
  11.3 358.1 %shard_map.178 = (bf16[4,2,128,768]{3,2,1,0:T(8,128)(2,1)}, f32[4,2,128,768]{3,2,1,0:T(8,128)}, f32[2,96,1536]{2,1,0:T(8,128)}, f32[2,96,768]{2,1,0:T(8,128)}, f...) custom-call(s32[1,1024]{1,0:T(1,128)} %keep_ref.1, ...), custom_call_target="tpu_custom_call" | custom-call | tf_op jit(solution)/shard_map/pallas_call | solution.py:865
  369.4 1.1 slice.24
  370.4 0.0 copy-start.2
  370.5 0.2 copy.30
  370.7 1.1 copy.32
  371.8 0.0 copy-start.3
  371.8 1.1 slice_bitcast_fusion.1
  372.8 0.0 copy-start.1
  372.8 0.8 copy.33
  373.7 0.0 copy-done.2
  373.7 1.1 slice_bitcast_fusion
  374.8 0.0 copy-done.3
  374.8 0.1 reshape.66
  374.9 0.7 constant_dynamic-slice_fusion.2
  375.6 0.6 constant_dynamic-slice_fusion.1
  376.2 0.1 constant_dynamic-slice_fusion
  376.3 0.6 copy.34
  376.9 0.0 copy-done.1
  376.9 0.0 copy-start
  376.9 1.1 copy.37
  378.1 1.3 copy-done
  379.4 1.7 copy.38
  (7 shorter events, 0.1 us)
Async XLA Ops:
  370.4 3.2 copy-start.2
  371.8 3.0 copy-start.3
  372.8 4.1 %copy-start.1 = (bf16[4,2,128,768]{3,2,1,0:T(8,128)(2,1)S(1)}, bf16[4,2,128,768]{3,2,1,0:T(8,128)(2,1)}, u32[]{:S(2)}) copy-start(bf16[4,2,128,768]{3,2,1,0:T(8,128)(2,1)} %get-tuple-element.14) | copy-start | bytes 4718596
  376.9 2.5 copy-start

commit v2 on v1

--- a/solution.py
+++ b/solution.py
@@ -78,14 +78,14 @@
 
 
 class GradSum:
-    def __init__(self, n_dp, me, mp, order, grad, landing, send_sem, recv_sem, credit, first, out, out_sem):
+    def __init__(self, n_dp, me, mp, order, grad, landing, send_sem, recv_sem, credit, next_order, finish):
         self.me, self.mp, self.order = me, mp, order
         self.steps = len(order)
         self.counts = [n_dp >> (k + 1) for k in range(self.steps)]
         self.offsets = [sum(self.counts[:k]) for k in range(self.steps)]
         self.grad, self.landing = grad, landing
         self.send_sem, self.recv_sem, self.credit = send_sem, recv_sem, credit
-        self.first, self.out, self.out_sem = first, out, out_sem
+        self.next_order, self.finish = next_order, finish
         self.opened = set()
         self.taken = [0] * self.steps
 
@@ -114,7 +114,7 @@
         )
 
     def send(self, k, m):
-        if not self.first and k not in self.opened:
+        if self.next_order is None and k not in self.opened:
             pl.semaphore_wait(self.credit.at[k], 1)
         self.opened.add(k)
         self.copy(k, m).start()
@@ -122,9 +122,6 @@
     def start(self):
         for m in self.turn(0):
             self.send(0, m)
-
-    def result(self):
-        return pltpu.make_async_copy(self.grad.at[self.me], self.out, self.out_sem)
 
     def take(self, k, m):
         self.copy(k, m).wait()
@@ -133,12 +130,12 @@
         if k + 1 < self.steps and m % 2 == 1:
             self.send(k + 1, m // 2)
         self.taken[k] += 1
-        if self.first and self.taken[k] == self.counts[k]:
+        if self.next_order is not None and self.taken[k] == self.counts[k]:
             pl.semaphore_signal(
-                self.credit.at[k], inc=1, device_id=(flipped(self.me, [self.order[k]]), self.mp), device_id_type=MESH
+                self.credit.at[k], inc=1, device_id=(flipped(self.me, [self.next_order[k]]), self.mp), device_id_type=MESH
             )
         if sum(self.taken) == sum(self.counts):
-            self.result().start()
+            self.finish(self.grad)
 
 
 def spread(grad_sum, places, plan):
@@ -153,7 +150,8 @@
     bits = n_dp.bit_length() - 1
     block = width // n_dp
     slots = heads * LANES
-    qkv_cols = 3 * heads * HEAD
+    channels = heads * HEAD
+    attn_cols = 4 * channels
     last = layers - 1
 
     def kernel(
@@ -170,9 +168,13 @@
         wd_in,
         packed_out,
         gpatch_out,
-        gm_out,
-        ga_out,
-        vec_out,
+        qkv_out,
+        wo_out,
+        up_out,
+        down_out,
+        head_out,
+        bias_out,
+        row_out,
         spill_q,
         spill_k,
         spill_v,
@@ -194,6 +196,7 @@
         V,
         O,
         LSE,
+        HV,
         G0,
         GP0,
         QA,
@@ -208,6 +211,7 @@
         CSEND,
         DX,
         DQ,
+        HATS,
         DK,
         DV,
         GM,
@@ -217,6 +221,8 @@
         VEC,
         VLAND,
         STAGE,
+        QKV_STAGE,
+        WO_STAGE,
         load_sem,
         spill_sem,
         stage_sem,
@@ -255,7 +261,10 @@
             return pltpu.make_async_copy(source, target, load_sem.at[index])
 
         def load_attn(layer):
-            return [load(wq_in.at[layer], WQ, 0), load(wo_in.at[layer], WO, 1)]
+            return [
+                load(wq_in.at[layer], WQ.at[:, 0:channels], 0),
+                load(wo_in.at[layer], WO.at[0:channels], 1),
+            ]
 
         def load_mlp(layer):
             return [load(wu_in.at[layer], WU, 2), load(wd_in.at[layer], WD, 3)]
@@ -297,24 +306,22 @@
                 device_id_type=MESH,
             )
 
-        def to_gather(chunk):
-            slot = chunk % 2
+        def to_gather(turn):
             return pltpu.make_async_remote_copy(
                 src_ref=CSEND,
-                dst_ref=CBUF.at[slot],
-                send_sem=c_send.at[slot],
-                recv_sem=c_recv.at[slot],
+                dst_ref=CBUF.at[turn],
+                send_sem=c_send.at[turn],
+                recv_sem=c_recv.at[turn],
                 device_id=(dp, sibling),
                 device_id_type=MESH,
             )
 
         def put_part(chunk, values):
             PART[chunk] = values.reshape(2, HALF, width)
+            to_sibling(chunk).start()
 
         def send_part(phase, chunk):
-            copy = to_sibling(chunk)
-            copy.start()
-            copy.wait()
+            to_sibling(chunk).wait()
             PART[chunk, core] += DBUF[chunk % 2]
             to_across(phase, chunk).start()
 
@@ -322,13 +329,14 @@
             to_across(phase, chunk).wait()
             return PART[chunk, core] + YBUF[phase % 2, chunk]
 
-        def gather(chunk, own, target):
+        def open_gather(turn, own, target):
             CSEND[...] = own
-            copy = to_gather(chunk)
-            copy.start()
+            to_gather(turn).start()
             target[core] = own.astype(target.dtype)
-            copy.wait()
-            target[1 - core] = CBUF[chunk % 2].astype(target.dtype)
+
+        def close_gather(turn, target):
+            to_gather(turn).wait()
+            target[1 - core] = CBUF[turn].astype(target.dtype)
 
         def whole(ref, chunk):
             return ref[chunk].reshape(CHUNK, width)
@@ -337,13 +345,27 @@
             VEC[layer, row : row + 1, 0 : values.shape[1]] += values
 
         def rv(layer, row):
-            return rv_ref[layer, row : row + 1, :]
+            return rv_ref[row, layer : layer + 1, :]
 
         def hv(layer, row, head):
-            return hv_ref[layer, row : row + 1, head * LANES : (head + 1) * LANES]
-
-        def head_cols(values, head, first=0):
-            return values[:, first + head * LANES : first + (head + 1) * LANES]
+            return HV[row, layer : layer + 1, head * LANES : (head + 1) * LANES]
+
+        def swap_halves(tile):
+            return pltpu.roll(tile, HEAD, 1)
+
+        def apart_heads(values):
+            tiles = []
+            for head in range(heads):
+                tile = values[:, head // 2 * LANES : (head // 2 + 1) * LANES]
+                tiles.append((swap_halves(tile) if head % 2 else tile) * real)
+            return tiles
+
+        def joined_heads(tiles):
+            pairs = [
+                tiles[first] + swap_halves(tiles[first + 1]) if first + 1 < len(tiles) else tiles[first]
+                for first in range(0, len(tiles), 2)
+            ]
+            return jnp.concatenate([pair.astype(BF16) for pair in pairs], axis=1)
 
         def pack(chunk):
             rows = lax.broadcasted_iota(jnp.int32, (CHUNK, tokens), 0) + chunk * CHUNK
@@ -353,7 +375,7 @@
             alive = jnp.sum(classes, axis=-1, keepdims=True)
             LIVE[chunk] = jnp.broadcast_to(alive, (CHUNK, LANES))
             KA[chunk] = (classes + jnp.where(lane == EMPTY, 1.0 - alive, 0.0)).astype(BF16)
-            put_part(chunk, values)
+            PART[chunk] = values.reshape(2, HALF, width)
             X[0, chunk] = PART[chunk, core]
             hat, _ = norm_rows(values)
             A[chunk] = (hat * (1.0 + rv(0, 0)) + rv(0, 1)).astype(BF16).reshape(2, HALF, width)
@@ -363,18 +385,17 @@
             return jnp.where(is_class, -APART * (1.0 - KA[chunk].astype(F32)), 0.0)
 
         def project(layer, chunk):
-            raw = mm(whole(A, chunk), WQ[...])
-            apart = apart_of(chunk)
-            classes = KA[chunk].astype(F32)
+            normed = whole(A, chunk)
+            raw_q, raw_k, raw_v = (apart_heads(mt(normed, WQ[kind])) for kind in range(3))
+            apart = apart_of(chunk).astype(BF16)
+            classes = KA[chunk]
             ones = (lane == HEAD).astype(F32)
             for head in range(heads):
-                hat, _ = norm_head(head_cols(raw, head) + hv(layer, 0, head), real)
-                Q[head, chunk] = (
-                    (hat * (1.0 + hv(layer, 3, head)) + hv(layer, 5, head)).astype(BF16) + apart.astype(BF16)
-                )
-                hat, _ = norm_head(head_cols(raw, head, slots) + hv(layer, 1, head), real)
-                K[head, chunk + 1] = (hat * (1.0 + hv(layer, 4, head))).astype(BF16) + classes.astype(BF16)
-                V[head, chunk + 1] = (head_cols(raw, head, 2 * slots) + hv(layer, 2, head) + ones).astype(BF16)
+                hat, _ = norm_head(raw_q[head] + hv(layer, 0, head), real)
+                Q[head, chunk] = (hat * (1.0 + hv(layer, 3, head)) + hv(layer, 5, head)).astype(BF16) + apart
+                hat, _ = norm_head(raw_k[head] + hv(layer, 1, head), real)
+                K[head, chunk + 1] = (hat * (1.0 + hv(layer, 4, head))).astype(BF16) + classes
+                V[head, chunk + 1] = (raw_v[head] + hv(layer, 2, head) + ones).astype(BF16)
 
         def window(ref, head, chunk):
             return ref[head, pl.ds(chunk, WINDOW)].reshape(WINDOW * CHUNK, LANES)
@@ -389,7 +410,7 @@
                 LSE[layer, head, chunk] = jnp.log(total) * (1.0 / math.log(2.0))
                 out = (out * (1.0 / total)).T
                 O[head, chunk] = jnp.where(lane < HEAD, out, 0.0).astype(BF16)
-            joined = jnp.concatenate([O[head, chunk] for head in range(heads)], axis=1)
+            joined = joined_heads([O[head, chunk].astype(F32) for head in range(heads)])
             put_part(chunk, mm(joined, WO[...]))
 
         def attn_forward(layer, phase):
@@ -403,7 +424,8 @@
                         X[layer, i] = x
                         hat, _ = norm_rows(x)
                         own = (hat * (1.0 + rv(layer, 0)) + rv(layer, 1)).astype(BF16).astype(F32)
-                        gather(i, own, A.at[i])
+                        open_gather(i % 2, own, A.at[i])
+                        close_gather(i % 2, A.at[i])
                     project(layer, i)
 
                 @pl.when(i > 0)
@@ -420,7 +442,8 @@
             X1[layer, chunk] = x1
             hat, _ = norm_rows(x1)
             own = (hat * (1.0 + rv(layer, 2)) + rv(layer, 3)).astype(BF16).astype(F32)
-            gather(chunk, own, target)
+            open_gather(chunk % 2, own, target)
+            close_gather(chunk % 2, target)
 
         def up(layer, second):
             before = mm(second, WU[...]) + ub_ref[layer : layer + 1, :]
@@ -440,10 +463,12 @@
 
             lax.fori_loop(0, chunks, slot, 0)
 
-        def mlp_grads(layer, second, act, grad_out, grad_before):
+        def up_grads(layer, second, grad_before):
             GM[layer, :, :, 0:hidden] += tm(second, grad_before).reshape(n_dp, block, hidden)
+            add_vec(layer, UP_BIAS_ROW, column_sum(grad_before.astype(F32)))
+
+        def down_grads(layer, act, grad_out):
             GM[layer, :, :, hidden:] += tm(grad_out, act).reshape(n_dp, block, hidden)
-            add_vec(layer, UP_BIAS_ROW, column_sum(grad_before.astype(F32)))
 
         def pump(name, i):
             for (where, index), events in plan.items():
@@ -476,8 +501,9 @@
                 grad = grad.astype(BF16)
                 grad_before = (mt(grad, WD[...]) * slope).astype(BF16)
                 put_part(i, mt(grad_before, WU[...]))
+                up_grads(layer, second, grad_before)
+                down_grads(layer, act, grad)
                 send_part(phase, i)
-                mlp_grads(layer, second, act, grad, grad_before)
                 return carry
 
             lax.fori_loop(0, chunks, slot, 0)
@@ -498,23 +524,30 @@
                 DX[i] = grad
                 own = grad.astype(BF16).astype(F32)
                 add_vec(layer, 5, column_sum(own))
-                gather(i, own, CT.at[0])
-                grad = whole(CT, 0)
-                grad_before = (mt(grad, WD[...]) * GP0[i].astype(F32)).astype(BF16)
+                turn = i % 2
+                open_gather(turn, own, CT.at[turn])
+
+                @pl.when(i > 0)
+                def _():
+                    down_grads(layer, G0[i - 1], whole(CT, 1 - turn))
+
+                close_gather(turn, CT.at[turn])
+                grad_before = (mt(whole(CT, turn), WD[...]) * GP0[i].astype(F32)).astype(BF16)
                 put_part(i, mt(grad_before, WU[...]))
+                up_grads(layer, whole(C0, i), grad_before)
                 send_part(phase, i)
-                mlp_grads(layer, whole(C0, i), G0[i], grad, grad_before)
                 pump(name, i)
                 return carry
 
             lax.fori_loop(0, chunks, slot, 0)
+            down_grads(layer, G0[chunks - 1], whole(CT, (chunks - 1) % 2))
 
         def attend_back(layer, chunk):
-            grad = whole(CT, 0)
-            grad_heads = mt(grad, WO[...]).astype(BF16)
+            grad = whole(CT, chunk % 2)
+            grad_heads = [tile.astype(BF16) for tile in apart_heads(mt(grad, WO[...]))]
             ring = chunk % WINDOW
             for head in range(heads):
-                grad_o = head_cols(grad_heads, head)
+                grad_o = grad_heads[head]
                 query = Q[head, chunk]
                 keys, values = window(K, head, chunk), window(V, head, chunk)
                 delta = column_sum((O[head, chunk].astype(F32) * grad_o.astype(F32)).T)
@@ -532,20 +565,26 @@
                     else:
                         DV[head, place] = grad_v[rows]
                         DK[head, place] = grad_k[rows]
+
+        def between_back(layer, chunk):
             out = [O[head, chunk].astype(F32) for head in range(heads)]
-            pairs = [pltpu.roll(out[0], HEAD, 1), out[1] + pltpu.roll(out[2], HEAD, 1)]
-            packed = jnp.concatenate(pairs, axis=1).astype(BF16)
-            GA[layer, :, :, qkv_cols - HEAD :] += tm(grad, packed).reshape(n_dp, block, 2 * LANES)
+            packed = joined_heads([jnp.zeros_like(out[0])] + out)
+            grad = whole(CT, chunk % 2)
+            GA[layer, :, :, attn_cols - 2 * LANES :] += tm(grad, packed).reshape(n_dp, block, 2 * LANES)
+            normed = whole(A, chunk)
+            for kind in range(2):
+                for head, raw in enumerate(apart_heads(mt(normed, WQ[kind]))):
+                    hat, rstd = norm_head(raw + hv(layer, kind, head), real)
+                    HATS[kind, head] = jnp.where(lane < HEAD, hat, rstd)
 
         def project_back(layer, chunk):
-            normed = whole(A, chunk)
-            raw = mm(normed, WQ[:, 0 : 2 * slots])
             ring, turn = chunk % WINDOW, chunk % 2
-            parts = [None] * (3 * heads)
+            parts = [[], [], []]
             for head in range(heads):
                 cols = head * LANES
                 for kind, grad in ((0, DQ[turn, head]), (1, DK[head, ring] * SCALE)):
-                    hat, rstd = norm_head(head_cols(raw, head, kind * slots) + hv(layer, kind, head), real)
+                    both = HATS[kind, head]
+                    hat, rstd = both * real, both[:, HEAD : HEAD + 1]
                     gain = (1.0 + hv(layer, 3 + kind, head)) * real
                     inner = norm_head_back(grad * gain, hat, rstd, real)
                     sums = [(HEAD_ROW + kind, inner), (HEAD_ROW + 3 + kind, grad * hat)]
@@ -553,24 +592,20 @@
                         sums.append((HEAD_ROW + 5, grad))
                     for row, values in sums:
                         VEC[layer, row : row + 1, cols : cols + LANES] += column_sum(values)
-                    parts[kind * heads + head] = inner
+                    parts[kind].append(inner)
                 grad_v = DV[head, ring]
                 VEC[layer, HEAD_ROW + 2 : HEAD_ROW + 3, cols : cols + LANES] += column_sum(grad_v)
-                parts[2 * heads + head] = grad_v
-            padded = jnp.concatenate([part.astype(BF16) for part in parts], axis=1)
-            put_part(chunk, mt(padded, WQ[...]))
-            pairs = []
-            for first in range(0, len(parts), 2):
-                if first + 1 < len(parts):
-                    pairs.append(parts[first] + pltpu.roll(parts[first + 1], HEAD, 1))
-                else:
-                    pairs.append(parts[first])
-            dense = jnp.concatenate([pair.astype(BF16) for pair in pairs], axis=1)
+                parts[2].append(grad_v)
+            dense = [joined_heads(tiles) for tiles in parts]
+            put_part(chunk, sum(mm(dense[kind], WQ[kind]) for kind in range(3)))
+            pairs = [tiles[0] + swap_halves(tiles[1]) for tiles in parts]
+            pairs += [parts[0][2] + swap_halves(parts[1][2]), parts[2][2]]
             cols = len(pairs) * LANES
-            GA[layer, :, :, 0:cols] += tm(normed, dense).reshape(n_dp, block, cols)
+            packed = jnp.concatenate([pair.astype(BF16) for pair in pairs], axis=1)
+            GA[layer, :, :, 0:cols] += tm(whole(A, chunk), packed).reshape(n_dp, block, cols)
 
         def attn_backward(layer, phase, name):
-            GA[layer] = jnp.zeros((n_dp, block, qkv_cols + heads * HEAD), F32)
+            GA[layer] = jnp.zeros((n_dp, block, attn_cols), F32)
             DK[...] = jnp.zeros_like(DK)
             DV[...] = jnp.zeros_like(DV)
 
@@ -585,7 +620,15 @@
                     DX[i] = grad
                     own = grad.astype(BF16).astype(F32)
                     add_vec(layer, 4, column_sum(own))
-                    gather(i, own, CT.at[0])
+                    open_gather(i % 2, own, CT.at[i % 2])
+
+                @pl.when(i > 0)
+                def _():
+                    between_back(layer, i - 1)
+
+                @pl.when(i < chunks)
+                def _():
+                    close_gather(i % 2, CT.at[i % 2])
                     attend_back(layer, i)
 
                 @pl.when(i > 0)
@@ -600,27 +643,65 @@
 
         near_first = [1, 0] + list(range(2, bits)) if bits > 1 else list(range(bits))
 
-        def grad_sum(kind, layer):
+        def mlp_results(layer):
+            return [
+                pltpu.make_async_copy(GM.at[layer, dp, :, 0:hidden], up_out.at[layer], out_sem.at[layer, 0]),
+                pltpu.make_async_copy(GM.at[layer, dp, :, hidden:], down_out.at[layer], out_sem.at[layer, 1]),
+            ]
+
+        def attn_results(layer):
+            return [
+                pltpu.make_async_copy(QKV_STAGE.at[layer], qkv_out.at[layer], out_sem.at[layer, 2]),
+                pltpu.make_async_copy(WO_STAGE.at[layer], wo_out.at[layer], out_sem.at[layer, 3]),
+            ]
+
+        def finish_mlp(layer):
+            start(mlp_results(layer))
+
+        def finish_attn(layer):
+            tiles = [GA[layer, dp, :, t * LANES : (t + 1) * LANES] for t in range(attn_cols // LANES)]
+            thirds = [tiles[3], swap_halves(tiles[3]), tiles[4]]
+            for kind in range(3):
+                QKV_STAGE[layer, kind, :, 0:LANES] = tiles[kind]
+                QKV_STAGE[layer, kind, :, LANES:channels] = thirds[kind][:, 0 : channels - LANES]
+            later = swap_halves(tiles[5])
+            WO_STAGE[layer, 0:LANES, :] = jnp.where(lane < HEAD, swap_halves(tiles[4]), later).T
+            WO_STAGE[layer, LANES:channels, :] = later.T[0 : channels - LANES]
+            start(attn_results(layer))
+
+        low_first = list(range(bits))
+
+        def grad_sum(kind, layer, order, next_order):
             if kind == 0:
-                parts = (list(range(bits)), GM, RM, m_send, m_recv, credit_m, gm_out)
+                parts = (GM, RM, m_send, m_recv, credit_m, finish_mlp)
             else:
-                parts = (near_first, GA, RA, a_send, a_recv, credit_a, ga_out)
-            order, grad, landing, sends, recvs, credit, out = parts
+                parts = (GA, RA, a_send, a_recv, credit_a, finish_attn)
+            grad, landing, sends, recvs, credit, finish = parts
             return GradSum(
-                n_dp, dp, mp, order, grad.at[layer], landing, sends, recvs, credit, layer == last,
-                out.at[layer], out_sem.at[2 * layer + kind],
+                n_dp, dp, mp, order, grad.at[layer], landing, sends, recvs, credit, next_order,
+                lambda _: finish(layer),
             )
 
-        mlp_last, attn_last = grad_sum(0, last), grad_sum(1, last)
-        mlp_first, attn_first = grad_sum(0, 0), grad_sum(1, 0)
+        mlp_last = grad_sum(0, last, low_first, low_first)
+        attn_last = grad_sum(1, last, low_first, low_first)
+        mlp_first = grad_sum(0, 0, low_first, None)
+        attn_first = grad_sum(1, 0, low_first, None)
         plan = {}
-        spread(mlp_last, [("a1", 2), ("a1", 3), ("a1", 4), ("m0", 0), ("m0", 1), ("m0", 2), ("m0", 3)], plan)
-        spread(attn_last, [("m0", 2), ("m0", 3), ("a0", 0), ("a0", 1), ("a0", 2)], plan)
-        spread(mlp_first, [("a0", 3), ("a0", 4), ("end", 0), ("end", 1), ("end", 2), ("end", 3)], plan)
+        spread(mlp_last, [("a1", 1), ("a1", 3), ("m0", 0), ("m0", 0), ("m0", 2), ("m0", 2), ("a0", 0)], plan)
+        spread(attn_last, [("m0", 3), ("m0", 3), ("a0", 1), ("a0", 1), ("a0", 1), ("a0", 1), ("a0", 3)], plan)
+        spread(mlp_first, [("a0", 2), ("a0", 3), ("end", 1), ("end", 1), ("end", 3), ("end", 3), ("tail", 1)], plan)
+        spread(attn_first, [('end', 3), ('tail', 0), ('tail', 1), ('tail', 1), ('tail', 2), ('tail', 2), ('tail', 3)], plan)
 
         first_loads = [load(patches_in, INP, 4)]
         start(first_loads + load_attn(0) + load_mlp(0))
         VEC[...] = jnp.zeros_like(VEC)
+        WQ[:, channels:] = jnp.zeros((3, WQ.shape[1] - channels, width), BF16)
+        WO[channels:] = jnp.zeros((WO.shape[0] - channels, width), BF16)
+        for row in range(HEAD_VECTORS):
+            STAGE[0, 0, 0:layers, 0 : 2 * LANES] = jnp.zeros((layers, 2 * LANES), F32)
+            STAGE[0, 0, 0:layers, 0:channels] = hv_ref[row]
+            for head, tile in enumerate(apart_heads(STAGE[0, 0, 0:layers, 0 : 2 * LANES])):
+                HV[row, :, head * LANES : (head + 1) * LANES] = tile
         keep = jnp.broadcast_to(keep_ref[...].astype(F32), (8, tokens))
         earlier = lax.broadcasted_iota(jnp.int32, (tokens, tokens), 0)
         later = lax.broadcasted_iota(jnp.int32, (tokens, tokens), 1)
@@ -664,13 +745,11 @@
             rows = input_back(0, 7, i)
             reload = pltpu.make_async_copy(spill_y.at[i], PART.at[i], stage_sem.at[0])
             reload.start()
-            CSEND[...] = rows
-            copy = to_gather(i)
-            copy.start()
-            X1[0, i] = rows
-            copy.wait()
-            X[last, i] = CBUF[i % 2]
+            halves = X.at[:, i]
+            open_gather(i % 2, rows, halves)
             reload.wait()
+            to_sibling(i).start()
+            close_gather(i % 2, halves)
             send_part(7, i)
             pump("end", i)
             return carry
@@ -687,11 +766,6 @@
                 device_id_type=MESH,
             )
 
-        copy = vec_copy(0, (dp, sibling))
-        copy.start()
-        copy.wait()
-        VEC[:, 0:UP_BIAS_ROW, :] += VLAND[0, :, 0:UP_BIAS_ROW, :]
-
         def unpack(patch_chunk, stage):
             stage[...] = jnp.zeros(stage.shape, F32)
             place = TCOL[pl.ds(patch_chunk * CHUNK, CHUNK), 0:1].astype(jnp.int32)
@@ -699,8 +773,7 @@
             def add_slots(chunk, carry):
                 slot = lax.broadcasted_iota(jnp.int32, (CHUNK, CHUNK), 1) + chunk * CHUNK
                 chosen = (place == slot).astype(F32).astype(BF16)
-                own, other = X1[0, chunk], X[last, chunk]
-                rest = jnp.concatenate([jnp.where(core == 0, own, other), jnp.where(core == 0, other, own)], axis=0)
+                rest = jnp.concatenate([X[0, chunk], X[1, chunk]], axis=0)
                 for _ in range(3):
                     piece = rest.astype(BF16)
                     stage[...] += mm(chosen, piece).reshape(stage.shape)
@@ -712,51 +785,83 @@
         def patch_copy(patch_chunk, turn):
             return pltpu.make_async_copy(STAGE.at[turn], gpatch_out.at[patch_chunk], stage_sem.at[turn])
 
-        for patch_chunk in range(chunks):
-            turn = patch_chunk % 2
-            if patch_chunk >= 2:
-                patch_copy(patch_chunk - 2, turn).wait()
-            unpack(patch_chunk, STAGE.at[turn])
-            patch_copy(patch_chunk, turn).start()
-            if patch_chunk < bits:
-                copy = vec_copy(1 + patch_chunk, (flipped(dp, [patch_chunk]), mp))
-                copy.start()
-                copy.wait()
-                VEC[...] += VLAND[1 + patch_chunk]
-        for step in range(chunks, bits):
-            copy = vec_copy(1 + step, (flipped(dp, [step]), mp))
-            copy.start()
-            copy.wait()
-            VEC[...] += VLAND[1 + step]
-        vec_done = pltpu.make_async_copy(VEC, vec_out, out_sem.at[2 * layers])
-        vec_done.start()
-        for patch_chunk in range(max(0, chunks - 2), chunks):
-            patch_copy(patch_chunk, patch_chunk % 2).wait()
-
-        events = attn_first.events()
-
         def out_copy(chunk):
-            return pltpu.make_async_copy(A.at[chunk], packed_out.at[chunk], spill_sem.at[0])
-
-        def out_slot(i, carry):
-            rows = (X1[last, i] + total_of(7, i) + rv(last, 5)) * LIVE[i, pl.ds(core * HALF, HALF), 0:1]
-            gather(i, rows.astype(BF16).astype(F32), A.at[i])
-            out_copy(i).start()
-            return carry
-
-        lax.fori_loop(0, chunks, out_slot, 0)
-        for event in events:
-            attn_first.take(*event)
-
-        def out_wait(i, carry):
-            out_copy(i).wait()
-            return carry
-
-        lax.fori_loop(0, chunks, out_wait, 0)
-        vec_done.wait()
-        for finished in (mlp_last, attn_last, mlp_first, attn_first):
-            assert finished.taken == finished.counts
-            finished.result().wait()
+            return pltpu.make_async_copy(A.at[chunk], packed_out.at[chunk], spill_sem.at[chunk])
+
+        def chosen_part(values, share):
+            column = lax.broadcasted_iota(jnp.int32, (values.shape[1], LANES), 0)
+            wanted = lax.broadcasted_iota(jnp.int32, (values.shape[1], LANES), 1)
+            chosen = ((column == wanted + dp * share) & (wanted < share)).astype(F32).astype(BF16)
+            total, rest = 0.0, values
+            for _ in range(3):
+                piece = rest.astype(BF16)
+                total = total + mm(piece, chosen)
+                rest = rest - piece.astype(F32)
+            return total[:, 0:share]
+
+        def vec_results():
+            for layer in range(layers):
+                rows = chosen_part(VEC[layer, 0:UP_BIAS_ROW, :], block)
+                for row in range(ROW_VECTORS):
+                    row_out[row, layer : layer + 1, :] = rows[row : row + 1]
+                rows = chosen_part(VEC[layer, UP_BIAS_ROW : 2 * UP_BIAS_ROW, 0:hidden], hidden // n_dp)
+                bias_out[layer : layer + 1, :] = rows[0:1]
+                heads_joined = [
+                    VEC[layer, UP_BIAS_ROW : 2 * UP_BIAS_ROW, head * LANES : (head + 1) * LANES] * real for head in range(heads)
+                ]
+                heads_joined = jnp.concatenate(
+                    [heads_joined[0] + swap_halves(heads_joined[1]), heads_joined[2]], axis=1
+                )
+                rows = chosen_part(heads_joined, channels // n_dp)
+                for row in range(HEAD_VECTORS):
+                    place = HEAD_ROW - UP_BIAS_ROW + row
+                    head_out[row, layer : layer + 1, :] = rows[place : place + 1]
+
+        def vec_partner(step):
+            return (dp, sibling) if step == 0 else (flipped(dp, [step - 1]), mp)
+
+        def vec_step(step):
+            vec_copy(step, vec_partner(step)).wait()
+            if step == 0:
+                VEC[:, 0:UP_BIAS_ROW, :] += VLAND[0, :, 0:UP_BIAS_ROW, :]
+            else:
+                VEC[...] += VLAND[step]
+            if step < bits:
+                vec_copy(step + 1, vec_partner(step + 1)).start()
+            else:
+                vec_results()
+
+        def unpack_next(step):
+            turn = step % 2
+            if step >= 2:
+                patch_copy(step - 2, turn).wait()
+            unpack(step, STAGE.at[turn])
+            patch_copy(step, turn).start()
+
+        vec_copy(0, vec_partner(0)).start()
+        unpack_next(0)
+        for step in range(chunks):
+            if step <= bits:
+                vec_step(step)
+            for job, event in plan.get(("tail", step), []):
+                job.take(*event)
+            rows = (X1[last, step] + total_of(7, step) + rv(last, 5)) * LIVE[step, pl.ds(core * HALF, HALF), 0:1]
+            open_gather(step % 2, rows.astype(BF16).astype(F32), A.at[step])
+            if step + 1 < chunks:
+                unpack_next(step + 1)
+            close_gather(step % 2, A.at[step])
+            out_copy(step).start()
+        for step in range(chunks, bits + 1):
+            vec_step(step)
+
+        for step in range(max(0, chunks - 2), chunks):
+            patch_copy(step, step % 2).wait()
+        for step in range(chunks):
+            out_copy(step).wait()
+        for job in (mlp_last, attn_last, mlp_first, attn_first):
+            assert job.taken == job.counts
+        for layer in range(layers):
+            wait(mlp_results(layer) + attn_results(layer))
 
     return kernel
 
@@ -773,16 +878,10 @@
     block = width // n_dp
     attn_cols = 4 * channels
 
-    def padded(values, axis):
-        shape = values.shape
-        split = values.reshape(shape[:axis] + (heads, HEAD) + shape[axis + 1 :])
-        pads = [(0, 0)] * split.ndim
-        pads[axis + 1] = (0, LANES - HEAD)
-        return jnp.pad(split, pads).reshape(shape[:axis] + (slots,) + shape[axis + 1 :])
-
-    wq = padded(w_qkv, 3).transpose(0, 2, 1, 3).reshape(layers, width, 3 * slots)
-    wo = padded(w_out, 1)
-    hv = padded(head_vectors, 2)
+    channels_up = (heads + 1) // 2 * LANES
+    wq = jnp.transpose(w_qkv, (0, 1, 3, 2))
+    hv = jnp.transpose(head_vectors, (1, 0, 2))
+    rv = jnp.transpose(row_vectors, (1, 0, 2))
     any_space = pl.BlockSpec(memory_space=pl.ANY)
     vmem = pl.BlockSpec(memory_space=pltpu.VMEM)
     sds = jax.ShapeDtypeStruct
@@ -792,9 +891,13 @@
     out_shape = [
         sds((chunks, 2) + half, BF16),
         sds((chunks, 2) + half, F32),
-        sds((layers, block, 2 * hidden), F32),
-        sds((layers, block, attn_cols), F32),
-        sds((layers, VEC_ROWS, width), F32),
+        sds((layers, 3, block, channels), F32),
+        sds((layers, channels, block), F32),
+        sds((layers, block, hidden), F32),
+        sds((layers, block, hidden), F32),
+        sds((HEAD_VECTORS, layers, channels // n_dp), F32),
+        sds((layers, hidden // n_dp), F32),
+        sds((ROW_VECTORS, layers, block), F32),
         sds(head_chunks, BF16),
         sds(head_window, BF16),
         sds(head_window, BF16),
@@ -806,8 +909,8 @@
     dma = pltpu.SemaphoreType.DMA
     scratch = [
         v((tokens, width), BF16),
-        v((width, 3 * slots), BF16),
-        v((slots, width), BF16),
+        v((3, channels_up, width), BF16),
+        v((channels_up, width), BF16),
         v((width, hidden), BF16),
         v((hidden, width), BF16),
         v((layers, chunks) + half, F32),
@@ -820,6 +923,7 @@
         v(head_window, BF16),
         v(head_chunks, BF16),
         v((layers, heads, chunks, 1, CHUNK), F32),
+        v((HEAD_VECTORS, layers, slots), F32),
         v((chunks, CHUNK, hidden), BF16),
         v((chunks, CHUNK, hidden), BF16),
         v((chunks, CHUNK, LANES), BF16),
@@ -834,6 +938,7 @@
         v(half, F32),
         v((chunks,) + half, F32),
         v((2, heads, CHUNK, LANES), F32),
+        v((2, heads, CHUNK, LANES), F32),
         v((heads, WINDOW, CHUNK, LANES), F32),
         v((heads, WINDOW, CHUNK, LANES), F32),
         v((layers, n_dp, block, 2 * hidden), F32),
@@ -843,6 +948,8 @@
         v((layers, VEC_ROWS, width), F32),
         v((bits + 1, layers, VEC_ROWS, width), F32),
         v((2, 2) + half, F32),
+        v((layers, 3, block, channels), F32),
+        v((layers, channels, block), F32),
         dma((5,)),
         dma((5,)),
         dma((2,)),
@@ -860,42 +967,29 @@
         pltpu.SemaphoreType.REGULAR((bits,)),
         dma((bits + 1,)),
         dma((bits + 1,)),
-        dma((2 * layers + 1,)),
+        dma((layers, 4)),
     ]
     results = pl.pallas_call(
         make_kernel(n_dp, tokens, width, hidden, heads, layers),
         out_shape=out_shape,
         in_specs=[vmem] * 5 + [any_space] * 6,
-        out_specs=[any_space] * len(out_shape),
+        out_specs=[any_space] * 6 + [vmem] * 3 + [any_space] * (len(out_shape) - 9),
         scratch_shapes=scratch,
         compiler_params=pltpu.CompilerParams(
             collective_id=0, has_side_effects=True, vmem_limit_bytes=64 * 2**20 - 2**16
         ),
-    )(patch_keep, patch_segment, hv, up_bias, row_vectors, patches, cotangent, wq, wo, w_up, w_down)
-    packed, grad_patches, gm, ga, vec = results[:5]
-
-    place = lax.axis_index("dp")
-
-    def mine(values):
-        share = values.shape[-1] // n_dp
-        return lax.dynamic_slice_in_dim(values, place * share, share, axis=values.ndim - 1)
-
-    grad_qkv = ga[:, :, : 3 * channels].reshape(layers, block, 3, channels).transpose(0, 2, 1, 3)
-    grad_out = ga[:, :, 3 * channels :].transpose(0, 2, 1)
-    grad_up = gm[:, :, :hidden]
-    grad_down = gm[:, :, hidden:].transpose(0, 2, 1)
-    head_rows = vec[:, HEAD_ROW : HEAD_ROW + HEAD_VECTORS, :slots].reshape(layers, HEAD_VECTORS, heads, LANES)
-    head_grads = mine(head_rows[..., :HEAD].reshape(layers, HEAD_VECTORS, channels))
+    )(patch_keep, patch_segment, hv, up_bias, rv, patches, cotangent, wq, w_out, w_up, w_down)
+    packed, grad_patches, grad_qkv, grad_out, grad_up, grad_down, head_grads, bias_grads, row_grads = results[:9]
     return (
         packed.reshape(tokens, width),
         grad_patches.reshape(tokens, width),
         grad_qkv,
         grad_out,
         grad_up,
-        grad_down,
-        head_grads,
-        mine(vec[:, UP_BIAS_ROW, :hidden]),
-        mine(vec[:, 0:ROW_VECTORS, :]),
+        jnp.transpose(grad_down, (0, 2, 1)),
+        jnp.transpose(head_grads, (1, 0, 2)),
+        bias_grads,
+        jnp.transpose(row_grads, (1, 0, 2)),
     )
 
 

time: 382 us -> 312 us (0.82)
  Pallas kernels: 358 us -> 302 us
  local copies, waits for them, and re-layouts: 22.3 us -> 9.37 us
    pallas_call x1, Pallas kernels: 358 us -> 302 us  [body(): pl.pallas_call(make_kernel(n_dp, tokens, width, hidden, heads, layers), o...]
    reshape x6 -> x0, local copies, waits for them, and re-layouts: 5.34 us -> none  [the longest x1 3.8 us: body(): padded(w_qkv, 3).transpose(0, 2, 1, 3).reshape(layers, width, 3 * slots)]
    pad x3 -> x0, local copies, waits for them, and re-layouts: 4.03 us -> none  [padded(): jnp.pad(split, pads).reshape(shape[:axis] + (slots,) + shape[axis + 1:])]
    unnamed x14 -> x25, local copies, waits for them, and re-layouts: 8.01 us -> 9.37 us
where the time goes in v2:
time: 312 us
  Pallas kernels  302 us (97%)
  local copies, waits for them, and re-layouts  9.37 us (3%)
    pallas_call x1, Pallas kernels, body(): pl.pallas_call(make_kernel(n_dp, tokens, width, hidden, heads, layers), o...  302 us
    unnamed x25, local copies, waits for them, and re-layouts  9.37 us

profile of v2, /device:TPU:0, one launch (start us, length us, event | category | flops | bytes accessed | tf_op | source)
XLA Modules:
  0.0 311.8 jit_solution(4732242815361931016)
XLA Ops:
  0.6 301.7 %shard_map.178 = (bf16[4,2,128,768]{3,2,1,0:T(8,128)(2,1)}, f32[4,2,128,768]{3,2,1,0:T(8,128)}, f32[2,3,96,192]{3,2,1,0:T(8,128)}, f32[2,192,96]{2,1,0:T(8,128)}...) custom-call(s32[1,1024]{1,0:T(1,128)} %keep_ref.1, ...), custom_call_target="tpu_custom_call" | custom-call | tf_op jit(solution)/shard_map/pallas_call | solution.py:972
  302.4 0.0 copy-start
  302.4 2.8 copy.29
  305.2 0.0 copy-done
  305.2 0.0 copy-start.3
  305.2 0.0 copy-start.4
  305.2 1.7 copy.30
  306.9 0.0 copy-done.3
  306.9 0.0 copy-start.2
  306.9 0.0 copy-start.1
  306.9 0.8 copy.31
  307.7 0.0 copy-done.4
  307.7 0.0 copy-start.6
  307.7 0.0 copy-start.7
  307.7 0.0 copy-start.5
  307.7 0.7 copy.32
  308.4 0.0 copy-done.2
  308.4 0.8 copy.33
  309.2 0.0 copy-done.1
  309.2 0.8 copy.34
  310.0 0.0 copy-done.6
  310.0 0.6 copy.35
  310.6 0.0 copy-done.7
  310.6 0.6 copy.36
  311.2 0.0 copy-done.5
  311.2 0.6 copy.37
Async XLA Ops:
  302.4 2.8 copy-start
  305.2 1.7 copy-start.3
  305.2 2.5 copy-start.4
  306.9 1.5 copy-start.2
  306.9 2.3 copy-start.1
  307.7 2.3 copy-start.6
  307.7 2.9 copy-start.7
  307.7 3.5 %copy-start.5 = (f32[6,2,96]{2,1,0:T(2,128)S(1)}, f32[6,2,96]{2,1,0:T(2,128)}, u32[]{:S(2)}) copy-start(f32[6,2,96]{2,1,0:T(2,128)} %get-tuple-element.26) | copy-start | bytes 13828

commit v3 on v2

--- a/solution.py
+++ b/solution.py
@@ -49,18 +49,16 @@
     return rstd * (grad - mean_grad - hat * mean_cross)
 
 
-def head_mean(values):
-    return jnp.sum(values, axis=-1, keepdims=True) * (1.0 / HEAD)
-
-
-def norm_head(values, real):
-    center = (values - head_mean(values)) * real
-    rstd = lax.rsqrt(head_mean(center * center) + EPS)
-    return center * rstd, rstd
-
-
-def norm_head_back(grad, hat, rstd, real):
-    return (rstd * real) * (grad - head_mean(grad) - hat * head_mean(grad * hat))
+def pieces(values, count):
+    found, rest = [], values
+    for _ in range(count):
+        found.append(rest.astype(BF16))
+        rest = rest - found[-1].astype(F32)
+    return found
+
+
+def mm_exact(values, right, count):
+    return sum(mm(piece, right) for piece in pieces(values, count))
 
 
 def column_sum(values):
@@ -86,20 +84,19 @@
         self.grad, self.landing = grad, landing
         self.send_sem, self.recv_sem, self.credit = send_sem, recv_sem, credit
         self.next_order, self.finish = next_order, finish
-        self.opened = set()
-        self.taken = [0] * self.steps
+        self.after, self.taken = {}, set()
 
     def turn(self, k):
         return sorted(range(self.counts[k]), key=lambda m: (m % 2 == 0, -m))
 
     def events(self):
-        found = [(k, m) for k in range(self.steps) for m in self.turn(k)]
-        if self.steps == 3:
-            found = [(0, 3), (0, 1), (0, 2), (1, 1), (0, 0), (1, 0), (2, 0)]
-        return found
+        return [(k, m) for k in range(self.steps) for m in self.turn(k)]
 
     def later_bits(self, k, m):
         return [self.order[k + 1 + t] for t in range(self.steps - k - 1) if (m >> t) & 1]
+
+    def partner(self, k, order=None):
+        return (flipped(self.me, [(order or self.order)[k]]), self.mp)
 
     def copy(self, k, m):
         slot = self.offsets[k] + m
@@ -109,47 +106,94 @@
             dst_ref=self.landing.at[slot],
             send_sem=self.send_sem.at[slot],
             recv_sem=self.recv_sem.at[slot],
-            device_id=(flipped(self.me, [self.order[k]]), self.mp),
+            device_id=self.partner(k),
             device_id_type=MESH,
         )
 
-    def send(self, k, m):
-        if self.next_order is None and k not in self.opened:
+    def prepare(self, events):
+        taken, sent = set(), set()
+        for event in events:
+            taken.add(event)
+            sends = []
+            for step in range(1, self.steps):
+                for index in self.turn(step):
+                    before = {(j, 1 << (step - 1 - j) | index << (step - j)) for j in range(step)}
+                    if (step, index) not in sent and before <= taken:
+                        first = all(step != other for other, _ in sent)
+                        sends.append((step, index, first))
+                        sent.add((step, index))
+            k = event[0]
+            freed = sum(step == k for step, _ in taken) == self.counts[k]
+            self.after[event] = (sends, freed, len(taken) == sum(self.counts))
+
+    def send(self, k, m, first):
+        if first and self.next_order is None:
             pl.semaphore_wait(self.credit.at[k], 1)
-        self.opened.add(k)
         self.copy(k, m).start()
 
     def start(self):
-        for m in self.turn(0):
-            self.send(0, m)
+        for position, m in enumerate(self.turn(0)):
+            self.send(0, m, position == 0)
 
     def take(self, k, m):
+        sends, freed, done = self.after[k, m]
         self.copy(k, m).wait()
         block = flipped(self.me, self.later_bits(k, m))
         self.grad[block] += self.landing[self.offsets[k] + m]
-        if k + 1 < self.steps and m % 2 == 1:
-            self.send(k + 1, m // 2)
-        self.taken[k] += 1
-        if self.next_order is not None and self.taken[k] == self.counts[k]:
-            pl.semaphore_signal(
-                self.credit.at[k], inc=1, device_id=(flipped(self.me, [self.next_order[k]]), self.mp), device_id_type=MESH
-            )
-        if sum(self.taken) == sum(self.counts):
-            self.finish(self.grad)
-
-
-def spread(grad_sum, places, plan):
-    events = grad_sum.events()
-    for position, event in enumerate(events):
-        place = places[position * len(places) // len(events)]
-        plan.setdefault(place, []).append((grad_sum, event))
+        self.taken.add((k, m))
+        for step, index, first in sends:
+            self.send(step, index, first)
+        if self.next_order is not None and freed:
+            target = self.partner(k, self.next_order)
+            pl.semaphore_signal(self.credit.at[k], inc=1, device_id=target, device_id_type=MESH)
+        if done:
+            self.finish()
+
+
+TAKEN = {
+    (0, 1): [(("a1m", 1), (0, 3)), (("a1m", 2), (0, 1)), (("a1", 2), (0, 2)), (("a1", 3), (0, 0)), (("m0", 0), (1, 1)), (("m0", 2), (1, 0)), (("a0m", 0), (2, 0))],
+    (1, 1): [(("a1m", 1), (0, 3)), (("a1m", 2), (0, 1)), (("a1", 2), (0, 2)), (("a1", 3), (0, 0)), (("m0", 0), (1, 1)), (("m0", 2), (1, 0)), (("a0m", 1), (2, 0))],
+    (2, 1): [(("m0", 3), (0, 3)), (("a0m", 0), (0, 1)), (("a0", 0), (0, 2)), (("a0", 0), (1, 1)), (("a0m", 1), (0, 0)), (("a0", 4), (1, 0)), (("end", 2), (2, 0))],
+    (0, 0): [(("a0m", 2), (0, 3)), (("a0m", 3), (0, 1)), (("a0", 3), (0, 2)), (("a0", 4), (0, 0)), (("end", 2), (1, 1)), (("end", 3), (1, 0)), (("tail", 3), (2, 0))],
+    (1, 0): [(("a0m", 1), (0, 3)), (("a0m", 2), (0, 1)), (("a0m", 3), (0, 2)), (("a0", 3), (0, 0)), (("end", 1), (1, 1)), (("end", 2), (1, 0)), (("tail", 1), (2, 0))],
+    (2, 0): [(("end", 3), (0, 3)), (("end", 3), (0, 1)), (("tail", 1), (0, 2)), (("tail", 2), (0, 0)), (("tail", 2), (1, 1)), (("tail", 3), (1, 0)), (("tail", 4), (2, 0))],
+}
+PHASES = ["a1", "m0", "a0", "end", "tail"]
+NEAR_FIRST = {(0, 1): 0, (1, 1): 1, (2, 1): 0, (0, 0): 0, (1, 0): 1, (2, 0): 0}
+SPREAD = {
+    (0, 1): [("a1", 2), ("a1", 3), ("a1", 4), ("m0", 0), ("m0", 1), ("m0", 2), ("m0", 3)],
+    (1, 1): [("a1", 2), ("a1", 3), ("a1", 4), ("m0", 0), ("m0", 1), ("m0", 2), ("m0", 3)],
+    (2, 1): [("m0", 2), ("m0", 3), ("a0", 0), ("a0", 1), ("a0", 2)],
+    (0, 0): [("a0", 2), ("a0", 3), ("a0", 4), ("end", 0), ("end", 1), ("end", 2), ("end", 3), ("tail", 0)],
+    (1, 0): [("a0", 2), ("a0", 3), ("a0", 4), ("end", 0), ("end", 1), ("end", 2), ("end", 3), ("tail", 0)],
+    (2, 0): [("end", 2), ("end", 3), ("tail", 0), ("tail", 1), ("tail", 2), ("tail", 3), ("tail", 4)],
+}
+
+
+def comes_at(place):
+    phase, slot = place
+    return (PHASES.index(phase.removesuffix("m")), slot, not phase.endswith("m"))
+
+
+def plan_sums(sums, last):
+    plan = {}
+    for (kind, layer), job in sums.items():
+        events, which = job.events(), (kind, int(layer == last))
+        taken = TAKEN[which]
+        if len(taken) != len(events):
+            places = SPREAD[which]
+            taken = [(places[n * len(places) // len(events)], event) for n, event in enumerate(events)]
+        taken = sorted(taken, key=lambda entry: comes_at(entry[0]))
+        job.prepare([event for _, event in taken])
+        for place, event in taken:
+            plan.setdefault(place, []).append((job, event))
+    return plan
 
 
 def make_kernel(n_dp, tokens, width, hidden, heads, layers):
     chunks = tokens // CHUNK
     bits = n_dp.bit_length() - 1
     block = width // n_dp
-    slots = heads * LANES
     channels = heads * HEAD
     attn_cols = 4 * channels
     last = layers - 1
@@ -197,6 +241,7 @@
         O,
         LSE,
         HV,
+        BLOCKS,
         G0,
         GP0,
         QA,
@@ -210,13 +255,17 @@
         CBUF,
         CSEND,
         DX,
+        WOB,
+        OD,
         DQ,
         HATS,
         DK,
         DV,
-        GM,
+        GU,
+        GD,
         GA,
-        RM,
+        RU,
+        RD,
         RA,
         VEC,
         VLAND,
@@ -232,12 +281,13 @@
         y_recv,
         c_send,
         c_recv,
-        m_send,
-        m_recv,
-        a_send,
-        a_recv,
-        credit_m,
-        credit_a,
+        o_send,
+        o_recv,
+        w_send,
+        w_recv,
+        g_send,
+        g_recv,
+        credit,
         v_send,
         v_recv,
         out_sem,
@@ -247,12 +297,13 @@
         core = mp % 2
         sibling = mp + 1 - 2 * core
         across = (mp + 2) % 4
+        diagonal = (sibling + 2) % 4
 
         barrier = pltpu.get_barrier_semaphore()
-        for other in (sibling, across):
+        for other in (sibling, across, diagonal):
             pl.semaphore_signal(barrier, inc=1, device_id=(dp, other), device_id_type=MESH)
-        for bit in range(bits):
-            pl.semaphore_signal(barrier, inc=1, device_id=(flipped(dp, [bit]), mp), device_id_type=MESH)
+        for flips in [[bit] for bit in range(bits)] + [[0, 1]]:
+            pl.semaphore_signal(barrier, inc=1, device_id=(flipped(dp, flips), mp), device_id_type=MESH)
 
         lane = lax.broadcasted_iota(jnp.int32, (1, LANES), 1)
         real = (lane < HEAD).astype(F32)
@@ -260,11 +311,11 @@
         def load(source, target, index):
             return pltpu.make_async_copy(source, target, load_sem.at[index])
 
-        def load_attn(layer):
-            return [
-                load(wq_in.at[layer], WQ.at[:, 0:channels], 0),
-                load(wo_in.at[layer], WO.at[0:channels], 1),
-            ]
+        def load_wq(layer):
+            return load(wq_in.at[layer], WQ.at[:, 0:channels], 0)
+
+        def load_wo(layer):
+            return load(wo_in.at[layer], WO.at[0:channels], 1)
 
         def load_mlp(layer):
             return [load(wu_in.at[layer], WU, 2), load(wd_in.at[layer], WD, 3)]
@@ -347,8 +398,18 @@
         def rv(layer, row):
             return rv_ref[row, layer : layer + 1, :]
 
-        def hv(layer, row, head):
-            return HV[row, layer : layer + 1, head * LANES : (head + 1) * LANES]
+        def hv(layer, row):
+            return HV[row, layer : layer + 1, :]
+
+        def norm_heads(values):
+            center = values - mm_exact(values, BLOCKS[...], 3)
+            rstd = lax.rsqrt(mm_exact(center * center, BLOCKS[...], 2) + EPS)
+            return center * rstd, rstd
+
+        def norm_heads_back(grad, hat, rstd):
+            mean_grad = mm_exact(grad, BLOCKS[...], 2)
+            mean_cross = mm_exact(grad * hat, BLOCKS[...], 2)
+            return rstd * (grad - mean_grad - hat * mean_cross)
 
         def swap_halves(tile):
             return pltpu.roll(tile, HEAD, 1)
@@ -365,7 +426,7 @@
                 tiles[first] + swap_halves(tiles[first + 1]) if first + 1 < len(tiles) else tiles[first]
                 for first in range(0, len(tiles), 2)
             ]
-            return jnp.concatenate([pair.astype(BF16) for pair in pairs], axis=1)
+            return jnp.concatenate(pairs, axis=1)
 
         def pack(chunk):
             rows = lax.broadcasted_iota(jnp.int32, (CHUNK, tokens), 0) + chunk * CHUNK
@@ -386,21 +447,48 @@
 
         def project(layer, chunk):
             normed = whole(A, chunk)
-            raw_q, raw_k, raw_v = (apart_heads(mt(normed, WQ[kind])) for kind in range(3))
             apart = apart_of(chunk).astype(BF16)
             classes = KA[chunk]
             ones = (lane == HEAD).astype(F32)
-            for head in range(heads):
-                hat, _ = norm_head(raw_q[head] + hv(layer, 0, head), real)
-                Q[head, chunk] = (hat * (1.0 + hv(layer, 3, head)) + hv(layer, 5, head)).astype(BF16) + apart
-                hat, _ = norm_head(raw_k[head] + hv(layer, 1, head), real)
-                K[head, chunk + 1] = (hat * (1.0 + hv(layer, 4, head))).astype(BF16) + classes
-                V[head, chunk + 1] = (raw_v[head] + hv(layer, 2, head) + ones).astype(BF16)
+            hat, _ = norm_heads(mt(normed, WQ[0]) + hv(layer, 0))
+            for head, tile in enumerate(apart_heads(hat * (1.0 + hv(layer, 3)) + hv(layer, 5))):
+                Q[head, chunk] = tile.astype(BF16) + apart
+            hat, _ = norm_heads(mt(normed, WQ[1]) + hv(layer, 1))
+            for head, tile in enumerate(apart_heads(hat * (1.0 + hv(layer, 4)))):
+                K[head, chunk + 1] = tile.astype(BF16) + classes
+            for head, tile in enumerate(apart_heads(mt(normed, WQ[2]) + hv(layer, 2))):
+                V[head, chunk + 1] = (tile + ones).astype(BF16)
 
         def window(ref, head, chunk):
             return ref[head, pl.ds(chunk, WINDOW)].reshape(WINDOW * CHUNK, LANES)
 
+        def dq_rows(turn, head):
+            return pl.ds(pl.multiple_of((turn * heads + head) * CHUNK, CHUNK), CHUNK)
+
+        def dk_rows(head, place):
+            return pl.ds(pl.multiple_of((head * WINDOW + place) * CHUNK, CHUNK), CHUNK)
+
+        def sent_at(chunk, half):
+            return pl.multiple_of((chunk * 2 + half) * channels, HEAD)
+
+        def landed_at(source, chunk):
+            return pl.multiple_of((source * chunks + chunk) * channels, HEAD)
+
+        def o_copies(chunk):
+            return [
+                pltpu.make_async_remote_copy(
+                    src_ref=DQ.at[pl.ds(sent_at(chunk, half), channels)],
+                    dst_ref=DK.at[pl.ds(landed_at(source, chunk), channels)],
+                    send_sem=o_send.at[source, chunk],
+                    recv_sem=o_recv.at[source, chunk],
+                    device_id=(dp, other),
+                    device_id_type=MESH,
+                )
+                for source, (other, half) in enumerate(((sibling, 1 - core), (across, core), (diagonal, 1 - core)))
+            ]
+
         def attend(layer, chunk):
+            outs = []
             for head in range(heads):
                 keys, values = window(K, head, chunk), window(V, head, chunk)
                 scores = mt(keys, Q[head, chunk])
@@ -409,41 +497,89 @@
                 total = out[HEAD : HEAD + 1, :]
                 LSE[layer, head, chunk] = jnp.log(total) * (1.0 / math.log(2.0))
                 out = (out * (1.0 / total)).T
-                O[head, chunk] = jnp.where(lane < HEAD, out, 0.0).astype(BF16)
-            joined = joined_heads([O[head, chunk].astype(F32) for head in range(heads)])
-            put_part(chunk, mm(joined, WO[...]))
-
-        def attn_forward(layer, phase):
-            def slot(i, carry):
-                @pl.when(i < chunks)
-                def _():
-                    if layer == 0:
-                        pack(i)
-                    else:
-                        x = X1[layer - 1, i] + total_of(phase - 1, i) + rv(layer - 1, 5)
-                        X[layer, i] = x
-                        hat, _ = norm_rows(x)
-                        own = (hat * (1.0 + rv(layer, 0)) + rv(layer, 1)).astype(BF16).astype(F32)
-                        open_gather(i % 2, own, A.at[i])
-                        close_gather(i % 2, A.at[i])
-                    project(layer, i)
-
-                @pl.when(i > 0)
-                def _():
-                    attend(layer, i - 1)
-                    send_part(phase, i - 1)
-
-                return carry
-
-            lax.fori_loop(0, chunks + 1, slot, 0)
-
-        def middle(layer, phase, chunk, target):
-            x1 = X[layer, chunk] + total_of(phase - 1, chunk) + rv(layer, 4)
+                out = jnp.where(lane < HEAD, out, 0.0).astype(BF16)
+                O[head, chunk] = out
+                outs.append(out.astype(F32))
+            pair, third = outs[0] + swap_halves(outs[1]), outs[2]
+            for half in range(2):
+                first, row = sent_at(chunk, half), half * HALF
+                DQ[pl.ds(first, HALF)] = pair[row : row + HALF]
+                DQ[pl.ds(first + HALF, HALF // 2)] = third[row : row + HALF // 2] + swap_halves(
+                    third[row + HALF // 2 : row + HALF]
+                )
+            start(o_copies(chunk))
+
+        share = n_dp // 4
+
+        quarter_of = bit_of(dp, 0) + 2 * bit_of(dp, 1)
+        near = [[0], [1], [0, 1]]
+
+        def w_quarter(layer, holder, quarter):
+            if share >= 4:
+                return GA.at[layer, pl.ds(holder * share + quarter * (share // 4), share // 4)]
+            per = 4 // share
+            rows = pl.ds(pl.multiple_of(quarter % per * (block // per), 8), block // per)
+            return GA.at[layer, pl.ds(holder * share + quarter // per, 1), rows]
+
+        def w_copy(layer, step):
+            holder, target = (mp if step < 2 else across), (dp, sibling)
+            if step == 0:
+                target = (dp, across)
+            elif 2 <= step < 5:
+                target = (flipped(dp, near[step - 2]), mp)
+            if step in (1, 5):
+                part = GA.at[layer, pl.ds(holder * share, share)]
+            else:
+                part = w_quarter(layer, holder, quarter_of)
+            return pltpu.make_async_remote_copy(
+                src_ref=part,
+                dst_ref=part,
+                send_sem=w_send.at[layer, step],
+                recv_sem=w_recv.at[layer, step],
+                device_id=target,
+                device_id_type=MESH,
+            )
+
+        def open_w(layer):
+            GA[layer, pl.ds(mp * share, share)] = WO[0:channels].astype(F32).reshape(share, block, width)
+            w_copy(layer, 0).start()
+            w_copy(layer, 1).start()
+
+        def spread_w(layer):
+            w_copy(layer, 0).wait()
+            start([w_copy(layer, step) for step in (2, 3, 4)])
+
+        def forward_w(layer):
+            wait([w_copy(layer, step) for step in (1, 2, 3, 4)])
+            w_copy(layer, 5).start()
+
+        def close_w(layer):
+            w_copy(layer, 5).wait()
+            for holder in range(4):
+                rows = GA[layer, holder * share : (holder + 1) * share].reshape(channels, width).astype(BF16)
+                WOB[holder * LANES : (holder + 1) * LANES] = rows[0:LANES]
+                WOB[4 * LANES + holder * HEAD : 4 * LANES + (holder + 1) * HEAD] = rows[LANES:channels]
+
+        def attn_out(chunk):
+            wait(o_copies(chunk))
+            places = [(DQ, sent_at(chunk, core))] + [(DK, landed_at(source, chunk)) for source in range(3)]
+            thirds = []
+            for holder, (ref, first) in zip((mp, sibling, across, diagonal), places):
+                OD[holder] = ref[pl.ds(first, HALF)].astype(BF16)
+                both = ref[pl.ds(first + HALF, HALF // 2)]
+                thirds.append(jnp.concatenate([both * real, swap_halves(both) * real], axis=0))
+            chip = mp // 2
+            for place, (same, other) in ((chip, thirds[:2]), (1 - chip, thirds[2:])):
+                low, high = jnp.where(core == 0, same, other), jnp.where(core == 0, other, same)
+                OD[4 + place] = (low + swap_halves(high)).astype(BF16)
+            return mm(jnp.concatenate([OD[tile] for tile in range(6)], axis=1), WOB[...])
+
+        def open_middle(layer, chunk, turn, target):
+            x1 = X[layer, chunk] + attn_out(chunk) + rv(layer, 4)
             X1[layer, chunk] = x1
             hat, _ = norm_rows(x1)
             own = (hat * (1.0 + rv(layer, 2)) + rv(layer, 3)).astype(BF16).astype(F32)
-            open_gather(chunk % 2, own, target)
-            close_gather(chunk % 2, target)
+            open_gather(turn, own, target)
 
         def up(layer, second):
             before = mm(second, WU[...]) + ub_ref[layer : layer + 1, :]
@@ -451,24 +587,60 @@
             density = jnp.exp(before * before * -0.5) * (1.0 / math.sqrt(2.0 * math.pi))
             return (before * cdf).astype(BF16), cdf + before * density
 
-        def mlp_forward(layer, phase):
+        def forward_first():
             def slot(i, carry):
-                middle(layer, phase, i, C0.at[i])
-                act, slope = up(layer, whole(C0, i))
-                G0[i] = act
-                GP0[i] = slope.astype(BF16)
-                put_part(i, mm(act, WD[...]))
-                send_part(phase, i)
+                @pl.when(i == 1)
+                def _():
+                    spread_w(0)
+
+                @pl.when(i < chunks)
+                def _():
+                    pack(i)
+                    project(0, i)
+
+                @pl.when((i > 0) & (i <= chunks))
+                def _():
+                    attend(0, i - 1)
+
+                @pl.when(i == 2)
+                def _():
+                    forward_w(0)
+                    wait(load_mlp(0))
+                    close_w(0)
+
+                @pl.when(i == chunks)
+                def _():
+                    load_wo(last).wait()
+                    open_w(last)
+                    start([load_wq(last)] + cot_load)
+
+                @pl.when(i > chunks)
+                def _():
+                    start(spills(False))
+                    spread_w(last)
+
+                @pl.when(i >= 2)
+                def _():
+                    j = i - 2
+                    turn = j % 2
+                    open_middle(0, j, turn, C0.at[j])
+                    close_gather(turn, C0.at[j])
+                    act, slope = up(0, whole(C0, j))
+                    G0[j] = act
+                    GP0[j] = slope.astype(BF16)
+                    put_part(j, mm(act, WD[...]))
+                    send_part(0, j)
+
                 return carry
 
-            lax.fori_loop(0, chunks, slot, 0)
+            lax.fori_loop(0, chunks + 2, slot, 0)
 
         def up_grads(layer, second, grad_before):
-            GM[layer, :, :, 0:hidden] += tm(second, grad_before).reshape(n_dp, block, hidden)
+            GU[layer] += tm(second, grad_before).reshape(n_dp, block, hidden)
             add_vec(layer, UP_BIAS_ROW, column_sum(grad_before.astype(F32)))
 
         def down_grads(layer, act, grad_out):
-            GM[layer, :, :, hidden:] += tm(grad_out, act).reshape(n_dp, block, hidden)
+            GD[layer] += tm(grad_out, act).reshape(n_dp, block, hidden)
 
         def pump(name, i):
             for (where, index), events in plan.items():
@@ -479,34 +651,75 @@
                         for grad_sum, event in events:
                             grad_sum.take(*event)
 
-        def mlp_turn(layer, phase):
-            GM[layer] = jnp.zeros((n_dp, block, 2 * hidden), F32)
+        def mlp_turn(layer, phase, chunk):
+            second = whole(CT, 0)
+            act, slope = up(layer, second)
+
+            @pl.when(chunk > 0)
+            def _():
+                pltpu.make_async_copy(STAGE.at[0], spill_y.at[chunk - 1], stage_sem.at[0]).wait()
+
+            STAGE[0] = mm(act, WD[...]).reshape(2, HALF, width)
+            pltpu.make_async_copy(STAGE.at[0], spill_y.at[chunk], stage_sem.at[0]).start()
+            grad = INP[pl.ds(chunk * CHUNK, CHUNK), :].astype(F32) * LIVE[chunk, :, 0:1]
+            CT[1] = grad.astype(BF16).reshape(2, HALF, width)
+            own = CT[1, core].astype(F32)
+            DX[chunk] = own
+            add_vec(layer, 5, column_sum(own))
+            grad = grad.astype(BF16)
+            grad_before = (mt(grad, WD[...]) * slope).astype(BF16)
+            put_part(chunk, mt(grad_before, WU[...]))
+            up_grads(layer, second, grad_before)
+            down_grads(layer, act, grad)
+            send_part(phase, chunk)
+
+        def forward_last():
+            GU[last] = jnp.zeros((n_dp, block, hidden), F32)
+            GD[last] = jnp.zeros((n_dp, block, hidden), F32)
 
             def slot(i, carry):
-                middle(layer, phase, i, CT.at[0])
-                second = whole(CT, 0)
-                act, slope = up(layer, second)
-
-                @pl.when(i > 0)
-                def _():
-                    pltpu.make_async_copy(STAGE.at[0], spill_y.at[i - 1], stage_sem.at[0]).wait()
-
-                STAGE[0] = mm(act, WD[...]).reshape(2, HALF, width)
-                pltpu.make_async_copy(STAGE.at[0], spill_y.at[i], stage_sem.at[0]).start()
-                grad = INP[pl.ds(i * CHUNK, CHUNK), :].astype(F32) * LIVE[i, :, 0:1]
-                CT[1] = grad.astype(BF16).reshape(2, HALF, width)
-                own = CT[1, core].astype(F32)
-                DX[i] = own
-                add_vec(layer, 5, column_sum(own))
-                grad = grad.astype(BF16)
-                grad_before = (mt(grad, WD[...]) * slope).astype(BF16)
-                put_part(i, mt(grad_before, WU[...]))
-                up_grads(layer, second, grad_before)
-                down_grads(layer, act, grad)
-                send_part(phase, i)
+                j = i - 2
+                turn = 1 - (j // 2) * (1 - j % 2)
+
+                @pl.when(i < chunks)
+                def _():
+                    x = X1[last - 1, i] + total_of(0, i) + rv(last - 1, 5)
+                    X[last, i] = x
+                    hat, _ = norm_rows(x)
+                    own = (hat * (1.0 + rv(last, 0)) + rv(last, 1)).astype(BF16).astype(F32)
+                    early = (i % 2) * (1 - i // 2)
+                    open_gather(early, own, A.at[i])
+                    close_gather(early, A.at[i])
+
+                @pl.when(i == 1)
+                def _():
+                    forward_w(last)
+
+                @pl.when(i == 2)
+                def _():
+                    close_w(last)
+                    wait(load_mlp(last) + cot_load)
+
+                @pl.when(i >= 2)
+                def _():
+                    open_middle(last, j, turn, CT.at[0])
+
+                @pl.when(i < chunks)
+                def _():
+                    project(last, i)
+
+                @pl.when((i > 0) & (i <= chunks))
+                def _():
+                    attend(last, i - 1)
+
+                @pl.when(i >= 2)
+                def _():
+                    close_gather(turn, CT.at[0])
+                    mlp_turn(last, 1, j)
+
                 return carry
 
-            lax.fori_loop(0, chunks, slot, 0)
+            lax.fori_loop(0, chunks + 2, slot, 0)
             pltpu.make_async_copy(STAGE.at[0], spill_y.at[chunks - 1], stage_sem.at[0]).wait()
 
         def input_back(layer, phase, chunk):
@@ -517,7 +730,8 @@
             return DX[chunk] + norm_back(grad_normed * (1.0 + rv(layer, 0)), hat, rstd)
 
         def mlp_backward(layer, phase, name):
-            GM[layer] = jnp.zeros((n_dp, block, 2 * hidden), F32)
+            GU[layer] = jnp.zeros((n_dp, block, hidden), F32)
+            GD[layer] = jnp.zeros((n_dp, block, hidden), F32)
 
             def slot(i, carry):
                 grad = input_back(layer + 1, phase, i)
@@ -550,58 +764,52 @@
                 grad_o = grad_heads[head]
                 query = Q[head, chunk]
                 keys, values = window(K, head, chunk), window(V, head, chunk)
-                delta = column_sum((O[head, chunk].astype(F32) * grad_o.astype(F32)).T)
+                cross = O[head, chunk].astype(F32) * grad_o.astype(F32)
+                delta = sum(mt(jnp.ones((8, LANES), BF16), piece) for piece in pieces(cross, 2))[0:1]
                 probs = jnp.exp2(mt(keys, query) * EXP2_SCALE - LSE[layer, head, chunk])
                 grad_scores = (probs * (mt(values, grad_o) - delta)).astype(BF16)
                 grad_v = mm(probs.astype(BF16), grad_o)
                 grad_k = mm(grad_scores, query)
-                DQ[chunk % 2, head] = tm(grad_scores, keys) * SCALE
+                DQ[dq_rows(chunk % 2, head)] = tm(grad_scores, keys) * SCALE
                 for part in range(WINDOW):
                     place = (ring + part + WINDOW - 1) % WINDOW
                     rows = slice(part * CHUNK, (part + 1) * CHUNK)
                     if part < WINDOW - 1:
                         DV[head, place] += grad_v[rows]
-                        DK[head, place] += grad_k[rows]
+                        DK[dk_rows(head, place)] += grad_k[rows]
                     else:
                         DV[head, place] = grad_v[rows]
-                        DK[head, place] = grad_k[rows]
+                        DK[dk_rows(head, place)] = grad_k[rows]
 
         def between_back(layer, chunk):
             out = [O[head, chunk].astype(F32) for head in range(heads)]
-            packed = joined_heads([jnp.zeros_like(out[0])] + out)
+            packed = joined_heads([jnp.zeros_like(out[0])] + out).astype(BF16)
             grad = whole(CT, chunk % 2)
             GA[layer, :, :, attn_cols - 2 * LANES :] += tm(grad, packed).reshape(n_dp, block, 2 * LANES)
             normed = whole(A, chunk)
             for kind in range(2):
-                for head, raw in enumerate(apart_heads(mt(normed, WQ[kind]))):
-                    hat, rstd = norm_head(raw + hv(layer, kind, head), real)
-                    HATS[kind, head] = jnp.where(lane < HEAD, hat, rstd)
+                HATS[kind, 0], HATS[kind, 1] = norm_heads(mt(normed, WQ[kind]) + hv(layer, kind))
 
         def project_back(layer, chunk):
             ring, turn = chunk % WINDOW, chunk % 2
-            parts = [[], [], []]
-            for head in range(heads):
-                cols = head * LANES
-                for kind, grad in ((0, DQ[turn, head]), (1, DK[head, ring] * SCALE)):
-                    both = HATS[kind, head]
-                    hat, rstd = both * real, both[:, HEAD : HEAD + 1]
-                    gain = (1.0 + hv(layer, 3 + kind, head)) * real
-                    inner = norm_head_back(grad * gain, hat, rstd, real)
-                    sums = [(HEAD_ROW + kind, inner), (HEAD_ROW + 3 + kind, grad * hat)]
-                    if kind == 0:
-                        sums.append((HEAD_ROW + 5, grad))
-                    for row, values in sums:
-                        VEC[layer, row : row + 1, cols : cols + LANES] += column_sum(values)
-                    parts[kind].append(inner)
-                grad_v = DV[head, ring]
-                VEC[layer, HEAD_ROW + 2 : HEAD_ROW + 3, cols : cols + LANES] += column_sum(grad_v)
-                parts[2].append(grad_v)
-            dense = [joined_heads(tiles) for tiles in parts]
-            put_part(chunk, sum(mm(dense[kind], WQ[kind]) for kind in range(3)))
-            pairs = [tiles[0] + swap_halves(tiles[1]) for tiles in parts]
-            pairs += [parts[0][2] + swap_halves(parts[1][2]), parts[2][2]]
-            cols = len(pairs) * LANES
-            packed = jnp.concatenate([pair.astype(BF16) for pair in pairs], axis=1)
+            grad_q = joined_heads([DQ[dq_rows(turn, head)] * real for head in range(heads)])
+            grad_k = joined_heads([DK[dk_rows(head, ring)] * (real * SCALE) for head in range(heads)])
+            grad_v = joined_heads([DV[head, ring] for head in range(heads)])
+            parts = []
+            for kind, grad in enumerate((grad_q, grad_k)):
+                hat, rstd = HATS[kind, 0], HATS[kind, 1]
+                inner = norm_heads_back(grad * (1.0 + hv(layer, 3 + kind)), hat, rstd)
+                add_vec(layer, HEAD_ROW + kind, column_sum(inner))
+                add_vec(layer, HEAD_ROW + 3 + kind, column_sum(grad * hat))
+                parts.append(inner)
+            add_vec(layer, HEAD_ROW + 5, column_sum(grad_q))
+            add_vec(layer, HEAD_ROW + 2, column_sum(grad_v))
+            parts.append(grad_v)
+            put_part(chunk, sum(mm(part.astype(BF16), WQ[kind]) for kind, part in enumerate(parts)))
+            firsts = [part[:, 0:LANES] for part in parts]
+            third_q, third_k, third_v = (part[:, LANES:] for part in parts)
+            packed = jnp.concatenate(firsts + [third_q + swap_halves(third_k), third_v], axis=1).astype(BF16)
+            cols = packed.shape[1]
             GA[layer, :, :, 0:cols] += tm(whole(A, chunk), packed).reshape(n_dp, block, cols)
 
         def attn_backward(layer, phase, name):
@@ -631,6 +839,8 @@
                     close_gather(i % 2, CT.at[i % 2])
                     attend_back(layer, i)
 
+                pump(name + "m", i)
+
                 @pl.when(i > 0)
                 def _():
                     project_back(layer, i - 1)
@@ -643,20 +853,16 @@
 
         near_first = [1, 0] + list(range(2, bits)) if bits > 1 else list(range(bits))
 
-        def mlp_results(layer):
+        def results(layer, kinds):
+            pairs = [
+                (GU.at[layer, dp], up_out),
+                (GD.at[layer, dp], down_out),
+                (QKV_STAGE.at[layer], qkv_out),
+                (WO_STAGE.at[layer], wo_out),
+            ]
             return [
-                pltpu.make_async_copy(GM.at[layer, dp, :, 0:hidden], up_out.at[layer], out_sem.at[layer, 0]),
-                pltpu.make_async_copy(GM.at[layer, dp, :, hidden:], down_out.at[layer], out_sem.at[layer, 1]),
+                pltpu.make_async_copy(pairs[kind][0], pairs[kind][1].at[layer], out_sem.at[layer, kind]) for kind in kinds
             ]
-
-        def attn_results(layer):
-            return [
-                pltpu.make_async_copy(QKV_STAGE.at[layer], qkv_out.at[layer], out_sem.at[layer, 2]),
-                pltpu.make_async_copy(WO_STAGE.at[layer], wo_out.at[layer], out_sem.at[layer, 3]),
-            ]
-
-        def finish_mlp(layer):
-            start(mlp_results(layer))
 
         def finish_attn(layer):
             tiles = [GA[layer, dp, :, t * LANES : (t + 1) * LANES] for t in range(attn_cols // LANES)]
@@ -667,41 +873,46 @@
             later = swap_halves(tiles[5])
             WO_STAGE[layer, 0:LANES, :] = jnp.where(lane < HEAD, swap_halves(tiles[4]), later).T
             WO_STAGE[layer, LANES:channels, :] = later.T[0 : channels - LANES]
-            start(attn_results(layer))
-
-        low_first = list(range(bits))
-
-        def grad_sum(kind, layer, order, next_order):
-            if kind == 0:
-                parts = (GM, RM, m_send, m_recv, credit_m, finish_mlp)
-            else:
-                parts = (GA, RA, a_send, a_recv, credit_a, finish_attn)
-            grad, landing, sends, recvs, credit, finish = parts
+            start(results(layer, (2, 3)))
+
+        def order_of(kind, layer):
+            return near_first if NEAR_FIRST[kind, int(layer == last)] else list(range(bits))
+
+        def grad_sum(kind, layer):
+            order = order_of(kind, layer)
+            next_order = order_of(kind, 0) if layer == last else None
+            grad, landing = ((GU, RU), (GD, RD), (GA, RA))[kind]
+
+            def finish():
+                if kind < 2:
+                    start(results(layer, (kind,)))
+                else:
+                    finish_attn(layer)
+
             return GradSum(
-                n_dp, dp, mp, order, grad.at[layer], landing, sends, recvs, credit, next_order,
-                lambda _: finish(layer),
+                n_dp, dp, mp, order, grad.at[layer], landing, g_send.at[kind], g_recv.at[kind], credit.at[kind],
+                next_order, finish,
             )
 
-        mlp_last = grad_sum(0, last, low_first, low_first)
-        attn_last = grad_sum(1, last, low_first, low_first)
-        mlp_first = grad_sum(0, 0, low_first, None)
-        attn_first = grad_sum(1, 0, low_first, None)
-        plan = {}
-        spread(mlp_last, [("a1", 1), ("a1", 3), ("m0", 0), ("m0", 0), ("m0", 2), ("m0", 2), ("a0", 0)], plan)
-        spread(attn_last, [("m0", 3), ("m0", 3), ("a0", 1), ("a0", 1), ("a0", 1), ("a0", 1), ("a0", 3)], plan)
-        spread(mlp_first, [("a0", 2), ("a0", 3), ("end", 1), ("end", 1), ("end", 3), ("end", 3), ("tail", 1)], plan)
-        spread(attn_first, [('end', 3), ('tail', 0), ('tail', 1), ('tail', 1), ('tail', 2), ('tail', 2), ('tail', 3)], plan)
-
-        first_loads = [load(patches_in, INP, 4)]
-        start(first_loads + load_attn(0) + load_mlp(0))
+        sums = {(kind, layer): grad_sum(kind, layer) for layer in (last, 0) for kind in range(3)}
+        plan = plan_sums(sums, last)
+
+        first_loads = [load(patches_in, INP, 4), load_wq(0)]
+        cot_load = [load(cot_in, INP, 4)]
+        load_wo(0).start()
+        start(first_loads + load_mlp(0))
+        load_wo(0).wait()
+        pl.semaphore_wait(barrier, 4 + bits)
+        open_w(0)
+        load_wo(last).start()
         VEC[...] = jnp.zeros_like(VEC)
         WQ[:, channels:] = jnp.zeros((3, WQ.shape[1] - channels, width), BF16)
         WO[channels:] = jnp.zeros((WO.shape[0] - channels, width), BF16)
-        for row in range(HEAD_VECTORS):
-            STAGE[0, 0, 0:layers, 0 : 2 * LANES] = jnp.zeros((layers, 2 * LANES), F32)
-            STAGE[0, 0, 0:layers, 0:channels] = hv_ref[row]
-            for head, tile in enumerate(apart_heads(STAGE[0, 0, 0:layers, 0 : 2 * LANES])):
-                HV[row, :, head * LANES : (head + 1) * LANES] = tile
+        HV[...] = jnp.zeros_like(HV)
+        HV[:, :, 0:channels] = hv_ref[...]
+        across_lanes = lax.broadcasted_iota(jnp.int32, BLOCKS.shape, 0) // HEAD
+        same_head = across_lanes == lax.broadcasted_iota(jnp.int32, BLOCKS.shape, 1) // HEAD
+        BLOCKS[...] = jnp.where(same_head, 1.0 / HEAD, 0.0).astype(BF16)
         keep = jnp.broadcast_to(keep_ref[...].astype(F32), (8, tokens))
         earlier = lax.broadcasted_iota(jnp.int32, (tokens, tokens), 0)
         later = lax.broadcasted_iota(jnp.int32, (tokens, tokens), 1)
@@ -716,33 +927,28 @@
             for edge in (0, chunks + 1):
                 K[head, edge] = padding
                 V[head, edge] = jnp.zeros((CHUNK, LANES), BF16)
-        wait(first_loads + load_attn(0))
-        pl.semaphore_wait(barrier, 2 + bits)
-
-        attn_forward(0, 0)
-        cot_load = [load(cot_in, INP, 4)]
-        start(spills(False) + load_attn(1) + cot_load)
+        wait(first_loads)
+
+        forward_first()
+        wait(spills(False) + [load_wq(last)])
+        start(load_mlp(last))
+        forward_last()
+        start(load_mlp(0))
+        sums[0, last].start()
+        sums[1, last].start()
+        attn_backward(last, 2, "a1")
+        sums[2, last].start()
+        start(spills(True) + [load_wq(0), load_wo(0)])
         wait(load_mlp(0))
-        mlp_forward(0, 1)
-        wait(spills(False) + load_attn(1))
-        start(load_mlp(1))
-        attn_forward(1, 2)
-        wait(load_mlp(1) + cot_load)
-        mlp_turn(1, 3)
-        start(load_mlp(0))
-        mlp_last.start()
-        attn_backward(1, 4, "a1")
-        attn_last.start()
-        start(spills(True) + load_attn(0))
-        wait(load_mlp(0))
-        mlp_backward(0, 5, "m0")
-        mlp_first.start()
-        wait(spills(True) + load_attn(0))
-        attn_backward(0, 6, "a0")
-        attn_first.start()
+        mlp_backward(0, 3, "m0")
+        sums[0, 0].start()
+        sums[1, 0].start()
+        wait(spills(True) + [load_wq(0), load_wo(0)])
+        attn_backward(0, 4, "a0")
+        sums[2, 0].start()
 
         def end_slot(i, carry):
-            rows = input_back(0, 7, i)
+            rows = input_back(0, 5, i)
             reload = pltpu.make_async_copy(spill_y.at[i], PART.at[i], stage_sem.at[0])
             reload.start()
             halves = X.at[:, i]
@@ -750,7 +956,7 @@
             reload.wait()
             to_sibling(i).start()
             close_gather(i % 2, halves)
-            send_part(7, i)
+            send_part(5, i)
             pump("end", i)
             return carry
 
@@ -774,10 +980,8 @@
                 slot = lax.broadcasted_iota(jnp.int32, (CHUNK, CHUNK), 1) + chunk * CHUNK
                 chosen = (place == slot).astype(F32).astype(BF16)
                 rest = jnp.concatenate([X[0, chunk], X[1, chunk]], axis=0)
-                for _ in range(3):
-                    piece = rest.astype(BF16)
+                for piece in pieces(rest, 3):
                     stage[...] += mm(chosen, piece).reshape(stage.shape)
-                    rest = rest - piece.astype(F32)
                 return carry
 
             lax.fori_loop(0, patch_chunk + 1, add_slots, 0)
@@ -792,12 +996,7 @@
             column = lax.broadcasted_iota(jnp.int32, (values.shape[1], LANES), 0)
             wanted = lax.broadcasted_iota(jnp.int32, (values.shape[1], LANES), 1)
             chosen = ((column == wanted + dp * share) & (wanted < share)).astype(F32).astype(BF16)
-            total, rest = 0.0, values
-            for _ in range(3):
-                piece = rest.astype(BF16)
-                total = total + mm(piece, chosen)
-                rest = rest - piece.astype(F32)
-            return total[:, 0:share]
+            return mm_exact(values, chosen, 3)[:, 0:share]
 
         def vec_results():
             for layer in range(layers):
@@ -806,13 +1005,7 @@
                     row_out[row, layer : layer + 1, :] = rows[row : row + 1]
                 rows = chosen_part(VEC[layer, UP_BIAS_ROW : 2 * UP_BIAS_ROW, 0:hidden], hidden // n_dp)
                 bias_out[layer : layer + 1, :] = rows[0:1]
-                heads_joined = [
-                    VEC[layer, UP_BIAS_ROW : 2 * UP_BIAS_ROW, head * LANES : (head + 1) * LANES] * real for head in range(heads)
-                ]
-                heads_joined = jnp.concatenate(
-                    [heads_joined[0] + swap_halves(heads_joined[1]), heads_joined[2]], axis=1
-                )
-                rows = chosen_part(heads_joined, channels // n_dp)
+                rows = chosen_part(VEC[layer, UP_BIAS_ROW : 2 * UP_BIAS_ROW, 0 : HV.shape[2]], channels // n_dp)
                 for row in range(HEAD_VECTORS):
                     place = HEAD_ROW - UP_BIAS_ROW + row
                     head_out[row, layer : layer + 1, :] = rows[place : place + 1]
@@ -845,7 +1038,7 @@
                 vec_step(step)
             for job, event in plan.get(("tail", step), []):
                 job.take(*event)
-            rows = (X1[last, step] + total_of(7, step) + rv(last, 5)) * LIVE[step, pl.ds(core * HALF, HALF), 0:1]
+            rows = (X1[last, step] + total_of(5, step) + rv(last, 5)) * LIVE[step, pl.ds(core * HALF, HALF), 0:1]
             open_gather(step % 2, rows.astype(BF16).astype(F32), A.at[step])
             if step + 1 < chunks:
                 unpack_next(step + 1)
@@ -853,15 +1046,17 @@
             out_copy(step).start()
         for step in range(chunks, bits + 1):
             vec_step(step)
+        for job, event in plan.get(("tail", chunks), []):
+            job.take(*event)
 
         for step in range(max(0, chunks - 2), chunks):
             patch_copy(step, step % 2).wait()
         for step in range(chunks):
             out_copy(step).wait()
-        for job in (mlp_last, attn_last, mlp_first, attn_first):
-            assert job.taken == job.counts
+        for job in sums.values():
+            assert len(job.taken) == n_dp - 1
         for layer in range(layers):
-            wait(mlp_results(layer) + attn_results(layer))
+            wait(results(layer, range(4)))
 
     return kernel
 
@@ -873,7 +1068,6 @@
     heads = channels // HEAD
     hidden = w_up.shape[2]
     chunks = tokens // CHUNK
-    slots = heads * LANES
     bits = n_dp.bit_length() - 1
     block = width // n_dp
     attn_cols = 4 * channels
@@ -923,7 +1117,8 @@
         v(head_window, BF16),
         v(head_chunks, BF16),
         v((layers, heads, chunks, 1, CHUNK), F32),
-        v((HEAD_VECTORS, layers, slots), F32),
+        v((HEAD_VECTORS, layers, channels_up), F32),
+        v((channels_up, channels_up), BF16),
         v((chunks, CHUNK, hidden), BF16),
         v((chunks, CHUNK, hidden), BF16),
         v((chunks, CHUNK, LANES), BF16),
@@ -937,13 +1132,17 @@
         v((2,) + half, F32),
         v(half, F32),
         v((chunks,) + half, F32),
-        v((2, heads, CHUNK, LANES), F32),
-        v((2, heads, CHUNK, LANES), F32),
+        v((width, width), BF16),
+        v((6, HALF, LANES), BF16),
+        v((2 * heads * CHUNK, LANES), F32),
+        v((2, 2, CHUNK, channels_up), F32),
+        v((heads * WINDOW * CHUNK, LANES), F32),
         v((heads, WINDOW, CHUNK, LANES), F32),
-        v((heads, WINDOW, CHUNK, LANES), F32),
-        v((layers, n_dp, block, 2 * hidden), F32),
+        v((layers, n_dp, block, hidden), F32),
+        v((layers, n_dp, block, hidden), F32),
         v((layers, n_dp, block, attn_cols), F32),
-        v((n_dp - 1, block, 2 * hidden), F32),
+        v((n_dp - 1, block, hidden), F32),
+        v((n_dp - 1, block, hidden), F32),
         v((n_dp - 1, block, attn_cols), F32),
         v((layers, VEC_ROWS, width), F32),
         v((bits + 1, layers, VEC_ROWS, width), F32),
@@ -959,12 +1158,13 @@
         dma((2, chunks)),
         dma((2,)),
         dma((2,)),
-        dma((n_dp - 1,)),
-        dma((n_dp - 1,)),
-        dma((n_dp - 1,)),
-        dma((n_dp - 1,)),
-        pltpu.SemaphoreType.REGULAR((bits,)),
-        pltpu.SemaphoreType.REGULAR((bits,)),
+        dma((3, chunks)),
+        dma((3, chunks)),
+        dma((layers, 6)),
+        dma((layers, 6)),
+        dma((3, n_dp - 1)),
+        dma((3, n_dp - 1)),
+        pltpu.SemaphoreType.REGULAR((3, bits)),
         dma((bits + 1,)),
         dma((bits + 1,)),
         dma((layers, 4)),

time: 312 us -> 299 us (0.958)
  Pallas kernels: 302 us -> 289 us
    pallas_call x1, Pallas kernels: 302 us -> 289 us  [body(): pl.pallas_call(make_kernel(n_dp, tokens, width, hidden, heads, layers), o...]
where the time goes in v3:
time: 299 us
  Pallas kernels  289 us (97%)
  local copies, waits for them, and re-layouts  9.37 us (3%)
    pallas_call x1, Pallas kernels, body(): pl.pallas_call(make_kernel(n_dp, tokens, width, hidden, heads, layers), o...  289 us
    unnamed x25, local copies, waits for them, and re-layouts  9.37 us

profile of v3, /device:TPU:0, one launch (start us, length us, event | category | flops | bytes accessed | tf_op | source)
XLA Modules:
  0.0 299.0 jit_solution(13852217722948248083)
XLA Ops:
  0.6 288.9 %shard_map.178 = (bf16[4,2,128,768]{3,2,1,0:T(8,128)(2,1)}, f32[4,2,128,768]{3,2,1,0:T(8,128)}, f32[2,3,96,192]{3,2,1,0:T(8,128)}, f32[2,192,96]{2,1,0:T(8,128)}...) custom-call(s32[1,1024]{1,0:T(1,128)} %keep_ref.1, ...), custom_call_target="tpu_custom_call" | custom-call | tf_op jit(solution)/shard_map/pallas_call | solution.py:1172
  289.6 0.0 copy-start
  289.6 2.8 copy.29
  292.4 0.0 copy-done
  292.4 0.0 copy-start.3
  292.4 0.0 copy-start.4
  292.4 1.7 copy.30
  294.1 0.0 copy-done.3
  294.1 0.0 copy-start.2
  294.1 0.0 copy-start.1
  294.1 0.8 copy.31
  294.9 0.0 copy-done.4
  294.9 0.0 copy-start.6
  294.9 0.0 copy-start.7
  294.9 0.0 copy-start.5
  294.9 0.7 copy.32
  295.6 0.0 copy-done.2
  295.6 0.8 copy.33
  296.4 0.0 copy-done.1
  296.4 0.8 copy.34
  297.2 0.0 copy-done.6
  297.2 0.6 copy.35
  297.8 0.0 copy-done.7
  297.8 0.6 copy.36
  298.4 0.0 copy-done.5
  298.4 0.6 copy.37
Async XLA Ops:
  289.6 2.8 copy-start
  292.4 1.7 copy-start.3
  292.4 2.5 copy-start.4
  294.1 1.5 copy-start.2
  294.1 2.3 copy-start.1
  294.9 2.3 copy-start.6
  294.9 2.9 copy-start.7
  294.9 3.5 %copy-start.5 = (f32[6,2,96]{2,1,0:T(2,128)S(1)}, f32[6,2,96]{2,1,0:T(2,128)}, u32[]{:S(2)}) copy-start(f32[6,2,96]{2,1,0:T(2,128)} %get-tuple-element.26) | copy-start | bytes 13828

commit v4 on v3

--- a/solution.py
+++ b/solution.py
@@ -587,6 +587,8 @@
             density = jnp.exp(before * before * -0.5) * (1.0 / math.sqrt(2.0 * math.pi))
             return (before * cdf).astype(BF16), cdf + before * density
 
+        LAG = 3
+
         def forward_first():
             def slot(i, carry):
                 @pl.when(i == 1)
@@ -602,7 +604,7 @@
                 def _():
                     attend(0, i - 1)
 
-                @pl.when(i == 2)
+                @pl.when(i == LAG)
                 def _():
                     forward_w(0)
                     wait(load_mlp(0))
@@ -614,14 +616,14 @@
                     open_w(last)
                     start([load_wq(last)] + cot_load)
 
-                @pl.when(i > chunks)
+                @pl.when(i == chunks + 1)
                 def _():
                     start(spills(False))
                     spread_w(last)
 
-                @pl.when(i >= 2)
-                def _():
-                    j = i - 2
+                @pl.when(i >= LAG)
+                def _():
+                    j = i - LAG
                     turn = j % 2
                     open_middle(0, j, turn, C0.at[j])
                     close_gather(turn, C0.at[j])
@@ -633,7 +635,7 @@
 
                 return carry
 
-            lax.fori_loop(0, chunks + 2, slot, 0)
+            lax.fori_loop(0, chunks + LAG, slot, 0)
 
         def up_grads(layer, second, grad_before):
             GU[layer] += tm(second, grad_before).reshape(n_dp, block, hidden)
@@ -678,8 +680,8 @@
             GD[last] = jnp.zeros((n_dp, block, hidden), F32)
 
             def slot(i, carry):
-                j = i - 2
-                turn = 1 - (j // 2) * (1 - j % 2)
+                j = i - LAG
+                turn = (i + LAG) % 2
 
                 @pl.when(i < chunks)
                 def _():
@@ -687,20 +689,19 @@
                     X[last, i] = x
                     hat, _ = norm_rows(x)
                     own = (hat * (1.0 + rv(last, 0)) + rv(last, 1)).astype(BF16).astype(F32)
-                    early = (i % 2) * (1 - i // 2)
-                    open_gather(early, own, A.at[i])
-                    close_gather(early, A.at[i])
+                    open_gather(i % 2, own, A.at[i])
+                    close_gather(i % 2, A.at[i])
 
                 @pl.when(i == 1)
                 def _():
                     forward_w(last)
 
-                @pl.when(i == 2)
+                @pl.when(i == LAG)
                 def _():
                     close_w(last)
                     wait(load_mlp(last) + cot_load)
 
-                @pl.when(i >= 2)
+                @pl.when(i >= LAG)
                 def _():
                     open_middle(last, j, turn, CT.at[0])
 
@@ -712,14 +713,14 @@
                 def _():
                     attend(last, i - 1)
 
-                @pl.when(i >= 2)
+                @pl.when(i >= LAG)
                 def _():
                     close_gather(turn, CT.at[0])
                     mlp_turn(last, 1, j)
 
                 return carry
 
-            lax.fori_loop(0, chunks + 2, slot, 0)
+            lax.fori_loop(0, chunks + LAG, slot, 0)
             pltpu.make_async_copy(STAGE.at[0], spill_y.at[chunks - 1], stage_sem.at[0]).wait()
 
         def input_back(layer, phase, chunk):

time: 299 us -> 286 us (0.957)
  Pallas kernels: 289 us -> 276 us
    pallas_call x1, Pallas kernels: 289 us -> 276 us  [body(): pl.pallas_call(make_kernel(n_dp, tokens, width, hidden, heads, layers), o...]
where the time goes in v4:
time: 286 us
  Pallas kernels  276 us (97%)
  local copies, waits for them, and re-layouts  9.37 us (3%)
    pallas_call x1, Pallas kernels, body(): pl.pallas_call(make_kernel(n_dp, tokens, width, hidden, heads, layers), o...  276 us
    unnamed x25, local copies, waits for them, and re-layouts  9.37 us

profile of v4, /device:TPU:0, one launch (start us, length us, event | category | flops | bytes accessed | tf_op | source)
XLA Modules:
  0.0 286.0 jit_solution(13057549839106276438)
XLA Ops:
  0.6 276.0 %shard_map.178 = (bf16[4,2,128,768]{3,2,1,0:T(8,128)(2,1)}, f32[4,2,128,768]{3,2,1,0:T(8,128)}, f32[2,3,96,192]{3,2,1,0:T(8,128)}, f32[2,192,96]{2,1,0:T(8,128)}...) custom-call(s32[1,1024]{1,0:T(1,128)} %keep_ref.1, ...), custom_call_target="tpu_custom_call" | custom-call | tf_op jit(solution)/shard_map/pallas_call | solution.py:1173
  276.6 0.0 copy-start
  276.6 2.8 copy.29
  279.4 0.0 copy-done
  279.4 0.0 copy-start.3
  279.4 0.0 copy-start.4
  279.4 1.7 copy.30
  281.1 0.0 copy-done.3
  281.1 0.0 copy-start.2
  281.1 0.0 copy-start.1
  281.1 0.8 copy.31
  281.9 0.0 copy-done.4
  281.9 0.0 copy-start.6
  281.9 0.0 copy-start.7
  281.9 0.0 copy-start.5
  281.9 0.7 copy.32
  282.6 0.0 copy-done.2
  282.6 0.8 copy.33
  283.4 0.0 copy-done.1
  283.4 0.8 copy.34
  284.2 0.0 copy-done.6
  284.3 0.6 copy.35
  284.8 0.0 copy-done.7
  284.8 0.6 copy.36
  285.4 0.0 copy-done.5
  285.4 0.6 copy.37
Async XLA Ops:
  276.6 2.8 copy-start
  279.4 1.7 copy-start.3
  279.4 2.5 copy-start.4
  281.1 1.5 copy-start.2
  281.1 2.3 copy-start.1
  281.9 2.3 copy-start.6
  281.9 2.9 %copy-start.7 = (f32[2,96]{1,0:T(2,128)S(1)}, f32[2,96]{1,0:T(2,128)}, u32[]{:S(2)}) copy-start(f32[2,96]{1,0:T(2,128)} %get-tuple-element.43) | copy-start | bytes 2308
  281.9 3.5 %copy-start.5 = (f32[6,2,96]{2,1,0:T(2,128)S(1)}, f32[6,2,96]{2,1,0:T(2,128)}, u32[]{:S(2)}) copy-start(f32[6,2,96]{2,1,0:T(2,128)} %get-tuple-element.26) | copy-start | bytes 13828

commit v5 on v4

--- a/solution.py
+++ b/solution.py
@@ -151,12 +151,12 @@
 
 
 TAKEN = {
-    (0, 1): [(("a1m", 1), (0, 3)), (("a1m", 2), (0, 1)), (("a1", 2), (0, 2)), (("a1", 3), (0, 0)), (("m0", 0), (1, 1)), (("m0", 2), (1, 0)), (("a0m", 0), (2, 0))],
-    (1, 1): [(("a1m", 1), (0, 3)), (("a1m", 2), (0, 1)), (("a1", 2), (0, 2)), (("a1", 3), (0, 0)), (("m0", 0), (1, 1)), (("m0", 2), (1, 0)), (("a0m", 1), (2, 0))],
-    (2, 1): [(("m0", 3), (0, 3)), (("a0m", 0), (0, 1)), (("a0", 0), (0, 2)), (("a0", 0), (1, 1)), (("a0m", 1), (0, 0)), (("a0", 4), (1, 0)), (("end", 2), (2, 0))],
-    (0, 0): [(("a0m", 2), (0, 3)), (("a0m", 3), (0, 1)), (("a0", 3), (0, 2)), (("a0", 4), (0, 0)), (("end", 2), (1, 1)), (("end", 3), (1, 0)), (("tail", 3), (2, 0))],
-    (1, 0): [(("a0m", 1), (0, 3)), (("a0m", 2), (0, 1)), (("a0m", 3), (0, 2)), (("a0", 3), (0, 0)), (("end", 1), (1, 1)), (("end", 2), (1, 0)), (("tail", 1), (2, 0))],
-    (2, 0): [(("end", 3), (0, 3)), (("end", 3), (0, 1)), (("tail", 1), (0, 2)), (("tail", 2), (0, 0)), (("tail", 2), (1, 1)), (("tail", 3), (1, 0)), (("tail", 4), (2, 0))],
+    (0, 1): [(("a1", 0), (0, 3)), (("a1", 1), (0, 1)), (("a1", 2), (0, 2)), (("a1", 3), (0, 0)), (("a1", 4), (1, 1)), (("m0", 1), (1, 0)), (("a0m", 0), (2, 0))],
+    (1, 1): [(("a1", 0), (0, 3)), (("a1", 1), (0, 1)), (("a1", 2), (0, 2)), (("a1", 3), (0, 0)), (("a1", 4), (1, 1)), (("m0", 1), (1, 0)), (("a0m", 1), (2, 0))],
+    (2, 1): [(("m0", 3), (0, 3)), (("a0m", 0), (0, 1)), (("a0m", 0), (0, 2)), (("a0m", 0), (1, 1)), (("a0m", 1), (0, 0)), (("a0", 4), (1, 0)), (("end", 2), (2, 0))],
+    (0, 0): [(("a0", 1), (0, 3)), (("a0", 2), (0, 1)), (("a0m", 3), (0, 2)), (("a0", 4), (0, 0)), (("end", 2), (1, 1)), (("end", 2), (1, 0)), (("tail", 2), (2, 0))],
+    (1, 0): [(("a0m", 1), (0, 3)), (("a0", 1), (0, 1)), (("a0", 2), (0, 2)), (("a0m", 3), (0, 0)), (("end", 0), (1, 1)), (("end", 2), (1, 0)), (("tail", 0), (2, 0))],
+    (2, 0): [(("end", 2), (0, 3)), (("end", 3), (0, 1)), (("tail", 0), (0, 2)), (("tail", 1), (0, 0)), (("tail", 1), (1, 1)), (("tail", 2), (1, 0)), (("tail", 4), (2, 0))],
 }
 PHASES = ["a1", "m0", "a0", "end", "tail"]
 NEAR_FIRST = {(0, 1): 0, (1, 1): 1, (2, 1): 0, (0, 0): 0, (1, 0): 1, (2, 0): 0}

time: 286 us -> 278 us (0.972)
  Pallas kernels: 276 us -> 267 us
    pallas_call x1, Pallas kernels: 276 us -> 267 us  [body(): pl.pallas_call(make_kernel(n_dp, tokens, width, hidden, heads, layers), o...]
where the time goes in v5:
time: 278 us
  Pallas kernels  267 us (96%)
  local copies, waits for them, and re-layouts  9.37 us (3%)
    pallas_call x1, Pallas kernels, body(): pl.pallas_call(make_kernel(n_dp, tokens, width, hidden, heads, layers), o...  267 us
    unnamed x25, local copies, waits for them, and re-layouts  9.37 us

profile of v5, /device:TPU:0, one launch (start us, length us, event | category | flops | bytes accessed | tf_op | source)
XLA Modules:
  0.0 277.5 jit_solution(8415786246443318234)
XLA Ops:
  0.6 267.5 %shard_map.178 = (bf16[4,2,128,768]{3,2,1,0:T(8,128)(2,1)}, f32[4,2,128,768]{3,2,1,0:T(8,128)}, f32[2,3,96,192]{3,2,1,0:T(8,128)}, f32[2,192,96]{2,1,0:T(8,128)}...) custom-call(s32[1,1024]{1,0:T(1,128)} %keep_ref.1, ...), custom_call_target="tpu_custom_call" | custom-call | tf_op jit(solution)/shard_map/pallas_call | solution.py:1173
  268.1 0.0 copy-start
  268.1 2.8 %copy.29 = bf16[1024,768]{1,0:T(8,128)(2,1)} copy(bf16[1024,768]{1,0:T(8,128)(2,1)} %bitcast.10) | data formatting | bytes 3145728
  270.9 0.0 copy-done
  270.9 0.0 copy-start.3
  270.9 0.0 copy-start.4
  270.9 1.7 copy.30
  272.6 0.0 copy-done.3
  272.6 0.0 copy-start.2
  272.6 0.0 copy-start.1
  272.6 0.8 copy.31
  273.4 0.0 copy-done.4
  273.4 0.0 copy-start.6
  273.4 0.0 copy-start.7
  273.4 0.0 copy-start.5
  273.4 0.7 copy.32
  274.1 0.0 copy-done.2
  274.1 0.8 copy.33
  274.9 0.0 copy-done.1
  274.9 0.8 copy.34
  275.7 0.0 copy-done.6
  275.7 0.6 copy.35
  276.3 0.0 copy-done.7
  276.3 0.6 copy.36
  276.9 0.0 copy-done.5
  276.9 0.6 copy.37
Async XLA Ops:
  268.1 2.8 %copy-start = (f32[4,2,128,768]{3,2,1,0:T(8,128)S(1)}, f32[4,2,128,768]{3,2,1,0:T(8,128)}, u32[]{:S(2)}) copy-start(f32[4,2,128,768]{3,2,1,0:T(8,128)} %get-tuple-element.19) | copy-start | bytes 9437188
  270.9 1.7 copy-start.3
  270.9 2.5 copy-start.4
  272.6 1.5 copy-start.2
  272.6 2.3 copy-start.1
  273.4 2.3 copy-start.6
  273.4 2.9 %copy-start.7 = (f32[2,96]{1,0:T(2,128)S(1)}, f32[2,96]{1,0:T(2,128)}, u32[]{:S(2)}) copy-start(f32[2,96]{1,0:T(2,128)} %get-tuple-element.43) | copy-start | bytes 2308
  273.4 3.5 %copy-start.5 = (f32[6,2,96]{2,1,0:T(2,128)S(1)}, f32[6,2,96]{2,1,0:T(2,128)}, u32[]{:S(2)}) copy-start(f32[6,2,96]{2,1,0:T(2,128)} %get-tuple-element.26) | copy-start | bytes 13828
